TPU v7x, 512 devices: a whole 4x4x16 slice. The times are simulated.
512 devices in a mesh: dom: 32 (over z, core), feat: 16 (over x, y).
Axes of the slice: x: 4, y: 4, z: 16, core: 2. Of those that a mesh axis runs over, the one named last changes fastest.
Arguments:
- grad_out: bfloat16 [512, 24576], P('feat', 'dom'), may hold values from -6 to 6
- saved_agg: bfloat16 [512, 24576], P('feat', 'dom'), may hold values from -0.09375 to 0.09375
- weight: bfloat16 [512, 512], P('feat'), may hold values from -0.25 to 0.25
- tile_values: bfloat16 [3072, 128, 128], P('dom'), may hold values from 0 to 0.029907227
- tile_dst: int32 [3072], P('dom'), may hold values from 0 to 5
- tile_slot: int32 [3072], P('dom'), may hold values from 0 to 31
- tile_count: int32 [32], P('dom'), may hold values from 12 to 96, as said below
- mirror_owner: int32 [32, 32], P('dom'), may hold values from 0 to 31, each once within a row
- mirror_local: int32 [32, 32], P('dom'), may hold values from 0 to 5
Outputs:
- grad_nodes: bfloat16 [512, 24576], P('feat', 'dom')
- grad_mirrors: bfloat16 [512, 131072], P('feat', 'dom')
- weight_grad: float32 [512, 512], P('feat')
Inputs may be any that keep to these rules, and one draw needn't show every extreme that they name: Every partition's first tile_count tiles are live, the rest are padding; some partition has all 96 live in every draw. `mirror_owner`: each partition's row names every partition once.
All inputs are finite; a program needn't handle non-finite values.
Results may differ from a plain program's by a relative error of at most 0.0049.
Values may be sent and summed in bfloat16 or wider, within the bound.
No kernel may reach another device: no remote copies, remote signals or barrier semaphores. Data moves between devices by JAX's collectives and lax.ppermute only.
A program may use at most 64 MiB of HBM per device.

v0:
```python
import jax
import jax.numpy as jnp
from jax import lax
from jax.sharding import PartitionSpec as P


def body(
    grad_out,
    saved_agg,
    weight,
    tile_values,
    tile_dst,
    tile_slot,
    tile_count,
    mirror_owner,
    mirror_local,
):
    row_count = grad_out.shape[0]
    vertices = grad_out.shape[1]
    block_count = vertices // 128
    peer_count = mirror_owner.shape[1]
    tile_total = tile_values.shape[0]
    piece = lax.all_gather(grad_out, "feat", axis=0, tiled=True)
    back_new = jnp.dot(weight, piece, preferred_element_type=jnp.float32)
    wgrad_part = lax.dot_general(
        saved_agg, piece, (((1,), (1,)), ((), ())), preferred_element_type=jnp.float32
    )
    weight_grad = lax.psum(wgrad_part, "dom")
    spread = back_new.astype(jnp.bfloat16).reshape(row_count, block_count, 128)
    dst_pick = (tile_dst[:, None] == jnp.arange(block_count, dtype=jnp.int32)[None, :]).astype(
        jnp.bfloat16
    )
    sources = jnp.einsum(
        "fbk,tb->tfk", spread, dst_pick, preferred_element_type=jnp.float32
    ).astype(jnp.bfloat16)
    products = jnp.einsum("tfk,tkj->tfj", sources, tile_values, preferred_element_type=jnp.float32)
    live_tiles = (jnp.arange(tile_total, dtype=jnp.int32) < tile_count[0]).astype(jnp.float32)
    slot_hot = (tile_slot[:, None] == jnp.arange(peer_count, dtype=jnp.int32)[None, :]).astype(
        jnp.float32
    )
    slot_hot = slot_hot * live_tiles[:, None]
    partial_value = jnp.einsum("tfj,ts->fsj", products, slot_hot, precision=lax.Precision.HIGHEST)
    owner_row = mirror_owner[0]
    local_row = mirror_local[0]
    target = owner_row * block_count + local_row
    place_hot = (
        target[:, None] == jnp.arange(peer_count * block_count, dtype=jnp.int32)[None, :]
    ).astype(jnp.float32)
    spread_all = jnp.einsum(
        "fsj,sg->fgj", partial_value, place_hot, precision=lax.Precision.HIGHEST
    )
    spread_all = spread_all.reshape(row_count, peer_count * block_count * 128)
    summed = lax.psum_scatter(spread_all, "dom", scatter_dimension=1, tiled=True)
    grad_nodes = summed.astype(jnp.bfloat16)
    all_nodes = lax.all_gather(grad_nodes, "dom", axis=1, tiled=True).reshape(
        row_count, peer_count * block_count, 128
    )
    mirrors = jnp.einsum(
        "fgj,sg->fsj", all_nodes, place_hot.astype(jnp.bfloat16), preferred_element_type=jnp.float32
    ).astype(jnp.bfloat16)
    grad_mirrors = mirrors.reshape(row_count, peer_count * 128)
    return (grad_nodes, grad_mirrors, weight_grad)


def solution(mesh):
    in_specs = (
        P("feat", "dom"),
        P("feat", "dom"),
        P("feat", None),
        P("dom", None, None),
        P("dom"),
        P("dom"),
        P("dom"),
        P("dom", None),
        P("dom", None),
    )
    out_specs = (P("feat", "dom"), P("feat", "dom"), P("feat", None))
    return jax.shard_map(body, mesh=mesh, in_specs=in_specs, out_specs=out_specs, check_vma=False)
```

profile of v0, /device:TPU:1, one launch (start us, length us, event | category | flops | bytes accessed | tf_op | source)
XLA Modules:
  0.0 422.0 jit_solution(7188025667522815927)
XLA Ops:
  7.2 0.0 copy-start
  7.2 0.0 copy-start.5
  7.2 0.0 copy-start.6
  7.2 0.0 copy-start.3
  7.2 0.0 reduce-scatter.2.cloned.1.call-start
  8.1 20.9 %all_gather.6 = bf16[512,768]{1,0:T(8,128)(2,1)S(1)} all-gather(bf16[32,768]{1,0:T(8,128)(2,1)} %param.9), channel_id=1, replica_groups=mesh['dom'=32,'feat'=16] {'feat'}, dimensions={0}, use_global_device_ids=true | all-gather | bytes 835584 | tf_op jit(solution)/shard_map/all_gather | solution.py:23
  28.9 0.9 copy-done.1
  29.8 1.0 convolution_convert_fusion.1
  30.8 0.1 reshape.38
  30.9 0.0 copy-done.5
  30.9 0.0 copy-done.6
  30.9 0.0 copy-done.3
  30.9 0.4 fusion.9
  31.4 0.0 copy-start.4
  31.4 1.0 fusion.5
  32.4 1.8 fusion.2
  34.2 1.5 fusion.12
  35.7 3.5 copy.25
  39.2 0.0 reduce-scatter.2.cloned.1.call-update
  39.2 0.0 all-gather.2.cloned.1.call-start
  39.2 115.8 %reduce-scatter.2.cloned.1.call-done = f32[32,768]{1,0:T(8,128)} async-done(((f32[32,24576]{1,0:T(8,128)}), f32[32,768]{1,0:T(8,128)}) %reduce-scatter.2.cloned.1.call-update) | async-done | bytes 98320 | tf_op jit(solution)/shard_map/reduce_scatter | solution.py:53
  155.0 1.5 convert_element_type.33
  156.6 0.0 all-gather.2.cloned.1.call-update
  156.6 0.0 all-reduce.2.cloned.1.call-start
  156.6 2.1 fusion.23
  158.8 0.0 all-reduce.2.cloned.1.call-update
  158.8 72.1 %all-gather.2.cloned.1.call-done = bf16[32,24576]{1,0:T(8,128)(2,1)} async-done(((bf16[32,768]{1,0:T(8,128)(2,1)}), bf16[32,24576]{1,0:T(8,128)(2,1)}) %all-gather.2.cloned.1.call-update) | async-done | bytes 1572880 | tf_op jit(solution)/shard_map/all_gather | solution.py:55
  230.9 1.8 copy.15
  232.7 0.4 convolution_convert_fusion
  233.1 0.8 copy.26
  234.0 180.0 %all-reduce.2.cloned.1.call-done = f32[32,512]{1,0:T(8,128)} async-done(((f32[32,512]{1,0:T(8,128)}), f32[32,512]{1,0:T(8,128)}) %all-reduce.2.cloned.1.call-update) | async-done | bytes 65552 | tf_op jit(solution)/shard_map/psum | solution.py:28
  414.0 1.5 copy.29
  (7 shorter events, 0.0 us)
Async XLA Ops:
  7.2 24.2 %copy-start = (bf16[96,128,128]{2,1,0:T(8,128)(2,1)S(1)}, bf16[96,128,128]{2,1,0:T(8,128)(2,1)}, u32[]{:S(2)}) copy-start(bf16[96,128,128]{2,1,0:T(8,128)(2,1)} %param.12) | copy-start | bytes 9437188
  7.2 23.7 %copy-start.5 = (s32[1,32]{1,0:T(1,128)S(1)}, s32[1,32]{1,0:T(1,128)}, u32[]{:S(2)}) copy-start(s32[1,32]{1,0:T(1,128)} %param.17) | copy-start | bytes 388
  7.2 23.7 %copy-start.6 = (s32[1,32]{1,0:T(1,128)S(1)}, s32[1,32]{1,0:T(1,128)}, u32[]{:S(2)}) copy-start(s32[1,32]{1,0:T(1,128)} %param.16) | copy-start | bytes 388
  7.2 23.7 %copy-start.3 = (s32[96]{0:T(128)S(1)}, s32[96]{0:T(128)}, u32[]{:S(2)}) copy-start(s32[96]{0:T(128)} %param.13) | copy-start | bytes 1156
  7.2 147.8 %reduce-scatter.2.cloned.1.call-start = ((), (), s32[]{:S(2)}) async-start(), calls=%async_computation.1 | async-start | bytes 3244032 | tf_op jit(solution)/shard_map/reduce_scatter | solution.py:53
  28.9 0.9 copy-start.1
  31.4 1.0 copy-start.4
  39.2 117.5 %copy-start.2 = (bf16[32,768]{1,0:T(8,128)(2,1)S(1)}, bf16[32,768]{1,0:T(8,128)(2,1)}, u32[]{:S(2)}) copy-start(bf16[32,768]{1,0:T(8,128)(2,1)} %param.10) | copy-start | bytes 147460
  39.2 191.7 %all-gather.2.cloned.1.call-start = ((), (), s32[]{:S(2)}) async-start(), calls=%async_computation.2 | async-start | bytes 1622016 | tf_op jit(solution)/shard_map/all_gather | solution.py:55
  156.6 257.4 %all-reduce.2.cloned.1.call-start = ((), (), s32[]{:S(2)}) async-start(), calls=%async_computation.3 | async-start | bytes 131072 | tf_op jit(solution)/shard_map/psum | solution.py:28
Sparse Core Ops, SparseCore 0:
  39.3 115.6 reduce-scatter.1
  158.0 72.8 all-gather.1
  233.9 180.0 all-reduce.1
where the time goes:
time: 422 us
  waiting for transfers between devices  368 us (87%)
  blocking collectives  20.9 us (5%)
  between operations  14.7 us (3%)
  local copies, waits for them, and re-layouts  8.52 us (2%)
  matrix products  8.27 us (2%)
    psum x1, waiting for transfers between devices, body(): weight_grad = lax.psum(wgrad_part, 'dom')  180 us
    reduce_scatter x1, waiting for transfers between devices, body(): lax.psum_scatter(spread_all, 'dom', scatter_dimension=1, tiled=True)  116 us
    all_gather x1, waiting for transfers between devices, body(): lax.all_gather(grad_nodes, 'dom', axis=1, tiled=True)  72.1 us
    all_gather x1, blocking collectives, body(): piece = lax.all_gather(grad_out, 'feat', axis=0, tiled=True)  20.9 us
  transfers between devices with their start and end apart: 3, of which 3 were waited for; matrix products, arithmetic and copies ran while one was open for 1% of the time, Pallas kernels for 0%

commit v1 on v0

v1 whole, which is shorter than its diff:
```python
import functools

import jax
import jax.numpy as jnp
from jax import lax
from jax.experimental import pallas as pl
from jax.experimental.pallas import tpu as pltpu
from jax.sharding import PartitionSpec as P

LANES = 128
UNROLL = 8
EXTRA = 8
VMEM_BYTES = 16 * 1024 * 1024


def partial_kernel(
    dst_ref, slot_ref, count_ref, owner_ref, local_ref,
    piece_ref, weight_ref, agg_ref, tiles_ref,
    msg_ref,
    back_ref, acc_ref, extra_ref,
):
    block_count, rows, _ = back_ref.shape
    peers = msg_ref.shape[0]
    tile_total = tiles_ref.shape[0]
    wide = weight_ref.shape[1] // LANES
    piece = piece_ref[...]
    back = jnp.dot(weight_ref[...], piece, preferred_element_type=jnp.float32)
    back = back.astype(jnp.bfloat16)
    for b in range(block_count):
        back_ref[b] = back[:, b * LANES : (b + 1) * LANES]
    acc_ref[...] = jnp.zeros_like(acc_ref)
    count = count_ref[0]

    def step(i, carry):
        products, places = [], []
        for u in range(UNROLL):
            t = i * UNROLL + u
            products.append(
                jnp.dot(back_ref[dst_ref[t]], tiles_ref[t], preferred_element_type=jnp.float32)
            )
            places.append(jnp.where(t < count, owner_ref[0, slot_ref[t]], peers))
        for place, product in zip(places, products):
            acc_ref[place] += product
        return carry

    lax.fori_loop(0, tile_total // UNROLL, step, 0)

    term = lax.dot_general(
        agg_ref[...], piece, (((1,), (1,)), ((), ())), preferred_element_type=jnp.float32
    )
    for k in range(wide):
        extra_ref[:, k, :] = term[:, k * LANES : (k + 1) * LANES]
    for k in range(wide, EXTRA):
        extra_ref[:, k, :] = jnp.zeros((peers, LANES), jnp.float32)

    def number(s, carry):
        value = local_ref[0, s].astype(jnp.float32)
        extra_ref[owner_ref[0, s], pl.ds(wide, 1), :] = jnp.full((1, LANES), value, jnp.float32)
        return carry

    lax.fori_loop(0, peers, number, 0)
    msg_ref[:, :rows, :] = acc_ref[:peers].astype(jnp.bfloat16)
    msg_ref[:, rows:, :] = extra_ref[...].astype(jnp.bfloat16)


def master_kernel(wide, got_ref, nodes_ref, msg_ref):
    peers, height, _ = got_ref.shape
    rows, columns = nodes_ref.shape
    block_count = columns // LANES
    tail = got_ref[:, rows:, :].astype(jnp.float32)
    numbers = [tail[p, wide : wide + 1, :] for p in range(peers)]
    sums = [jnp.zeros((rows, LANES), jnp.float32) for _ in range(block_count)]
    for p in range(peers):
        part = got_ref[p, :rows, :].astype(jnp.float32)
        for b in range(block_count):
            sums[b] = sums[b] + jnp.where(numbers[p] == float(b), part, 0.0)
    for b in range(block_count):
        nodes_ref[:, b * LANES : (b + 1) * LANES] = sums[b].astype(jnp.bfloat16)
    for p in range(peers):
        pick = sums[0]
        for b in range(1, block_count):
            pick = jnp.where(numbers[p] == float(b), sums[b], pick)
        msg_ref[p, :rows, :] = pick.astype(jnp.bfloat16)
    total = jnp.sum(tail, axis=0)
    high = total[:wide].astype(jnp.bfloat16)
    low = (total[:wide] - high.astype(jnp.float32)).astype(jnp.bfloat16)
    both = jnp.concatenate([high.astype(jnp.float32), low.astype(jnp.float32)], axis=0)
    both = both.astype(jnp.bfloat16)
    for p in range(peers):
        msg_ref[p, rows:, :] = both


def mirror_kernel(wide, owner_ref, got_ref, mirrors_ref, wgrad_ref):
    peers = got_ref.shape[0]
    rows = mirrors_ref.shape[0]
    for s in range(peers):
        mirrors_ref[:, s * LANES : (s + 1) * LANES] = got_ref[owner_ref[0, s], :rows, :]
    tail = got_ref[:, rows:, :].astype(jnp.float32)
    for k in range(wide):
        wgrad_ref[:, k * LANES : (k + 1) * LANES] = tail[:, k, :] + tail[:, wide + k, :]


def body(
    grad_out,
    saved_agg,
    weight,
    tile_values,
    tile_dst,
    tile_slot,
    tile_count,
    mirror_owner,
    mirror_local,
):
    rows, columns = grad_out.shape
    block_count = columns // LANES
    peers = mirror_owner.shape[1]
    features = weight.shape[1]
    wide = features // LANES
    groups = features // rows
    height = rows + EXTRA
    vmem = pl.BlockSpec(memory_space=pltpu.VMEM)
    smem = pl.BlockSpec(memory_space=pltpu.SMEM)
    params = pltpu.CompilerParams(vmem_limit_bytes=VMEM_BYTES)

    with jax.named_scope("gather_features"):
        copies = jnp.broadcast_to(grad_out[None], (groups, rows, columns))
        piece = lax.all_to_all(copies, "feat", 0, 0, tiled=True).reshape(features, columns)
    message = pl.pallas_call(
        partial_kernel,
        out_shape=jax.ShapeDtypeStruct((peers, height, LANES), jnp.bfloat16),
        in_specs=[smem] * 5 + [vmem] * 4,
        out_specs=vmem,
        scratch_shapes=[
            pltpu.VMEM((block_count, rows, LANES), jnp.bfloat16),
            pltpu.VMEM((peers + 1, rows, LANES), jnp.float32),
            pltpu.VMEM((peers, EXTRA, LANES), jnp.float32),
        ],
        compiler_params=params,
        name="partials",
    )(
        tile_dst, tile_slot, tile_count, mirror_owner, mirror_local,
        piece, weight, saved_agg, tile_values,
    )
    with jax.named_scope("to_masters"):
        got = lax.all_to_all(message, "dom", 0, 0, tiled=True)
    grad_nodes, answer = pl.pallas_call(
        functools.partial(master_kernel, wide),
        out_shape=(
            jax.ShapeDtypeStruct((rows, columns), jnp.bfloat16),
            jax.ShapeDtypeStruct((peers, height, LANES), jnp.bfloat16),
        ),
        in_specs=[vmem],
        out_specs=(vmem, vmem),
        compiler_params=params,
        name="masters",
    )(got)
    with jax.named_scope("to_mirrors"):
        back = lax.all_to_all(answer, "dom", 0, 0, tiled=True)
    grad_mirrors, weight_grad = pl.pallas_call(
        functools.partial(mirror_kernel, wide),
        out_shape=(
            jax.ShapeDtypeStruct((rows, peers * LANES), jnp.bfloat16),
            jax.ShapeDtypeStruct((rows, features), jnp.float32),
        ),
        in_specs=[smem, vmem],
        out_specs=(vmem, vmem),
        compiler_params=params,
        name="mirrors",
    )(mirror_owner, back)
    return (grad_nodes, grad_mirrors, weight_grad)


def solution(mesh):
    in_specs = (
        P("feat", "dom"),
        P("feat", "dom"),
        P("feat", None),
        P("dom", None, None),
        P("dom"),
        P("dom"),
        P("dom"),
        P("dom", None),
        P("dom", None),
    )
    out_specs = (P("feat", "dom"), P("feat", "dom"), P("feat", None))
    return jax.shard_map(body, mesh=mesh, in_specs=in_specs, out_specs=out_specs, check_vma=False)
```

time: 422 us -> 107 us (0.25)
  waiting for transfers between devices: 368 us -> 10 us
  blocking collectives: 20.9 us -> 73.3 us
  between operations: 14.7 us -> 1.32 us
  matrix products: 8.27 us -> 0 us
  starting transfers between devices: 0.12 us -> 7.58 us
  Pallas kernels: 0 us -> 5.95 us
    psum x1 -> x0, waiting for transfers between devices: 180 us -> none  [body(): weight_grad = lax.psum(wgrad_part, 'dom')]
    reduce_scatter x1 -> x0, waiting for transfers between devices: 116 us -> none  [body(): lax.psum_scatter(spread_all, 'dom', scatter_dimension=1, tiled=True)]
    all_to_all x0 -> x2, blocking collectives: none -> 73.3 us  [the longest x1 44.7 us: body(): got = lax.all_to_all(message, 'dom', 0, 0, tiled=True)]
    all_gather x1 -> x0, waiting for transfers between devices: 72.1 us -> none  [body(): lax.all_gather(grad_nodes, 'dom', axis=1, tiled=True)]
    all_gather x1 -> x0, blocking collectives: 20.9 us -> none  [body(): piece = lax.all_gather(grad_out, 'feat', axis=0, tiled=True)]
    all_to_all x0 -> x1, waiting for transfers between devices: none -> 10 us  [body(): lax.all_to_all(copies, 'feat', 0, 0, tiled=True).reshape(features, columns)]
    dot_general x7 -> x0, matrix products: 8.27 us -> none  [the longest x1 2.1 us: body(): lax.dot_general(saved_agg, piece, (((1,), (1,)), ((), ())), preferred_ele...]
    all_to_all x0 -> x1, starting transfers between devices: none -> 7.58 us  [body(): lax.all_to_all(copies, 'feat', 0, 0, tiled=True).reshape(features, columns)]
  transfers between devices with their start and end apart: 3 -> 1, of which waited for: 3 -> 1; matrix products, arithmetic and copies ran while one was open for 1% -> 0% of each run, Pallas kernels for 0% -> 0%
where the time goes in v1:
time: 107 us; the launch traced here: 106 us
  blocking collectives  73.3 us (69%)
  waiting for transfers between devices  10 us (9%)
  local copies, waits for them, and re-layouts  7.84 us (7%)
  starting transfers between devices  7.58 us (7%)
  Pallas kernels  5.95 us (6%)
  between operations  1.32 us (1%)
    all_to_all x1, blocking collectives, body(): got = lax.all_to_all(message, 'dom', 0, 0, tiled=True)  44.7 us
    all_to_all x1, blocking collectives, body(): back = lax.all_to_all(answer, 'dom', 0, 0, tiled=True)  28.6 us
    all_to_all x1, waiting for transfers between devices, body(): lax.all_to_all(copies, 'feat', 0, 0, tiled=True).reshape(features, columns)  10 us
    all_to_all x1, starting transfers between devices, body(): lax.all_to_all(copies, 'feat', 0, 0, tiled=True).reshape(features, columns)  7.58 us
    unnamed x16, local copies, waits for them, and re-layouts  6.07 us
    pallas_call x1, Pallas kernels, body(): pl.pallas_call(partial_kernel, out_shape=jax.ShapeDtypeStruct((peers, hei...  3.55 us
  transfers between devices with their start and end apart: 1, of which 1 were waited for; matrix products, arithmetic and copies ran while one was open for 0% of the time, Pallas kernels for 0%

profile of v1, /device:TPU:1, one launch (start us, length us, event | category | flops | bytes accessed | tf_op | source)
XLA Modules:
  0.0 106.0 jit_solution(2728797025759854428)
XLA Ops:
  0.6 1.8 %broadcast_in_dim.2 = bf16[16,32,768]{2,1,0:T(8,128)(2,1)} broadcast(bf16[32,768]{1,0:T(8,128)(2,1)} %param.9), dimensions={1,2} | broadcast | bytes 835584 | tf_op jit(solution)/shard_map/gather_features/broadcast_in_dim | solution.py:126
  2.4 7.6 %all-to-all-start = ((bf16[16,32,768]{2,1,0:T(8,128)(2,1)}), bf16[16,32,768]{2,1,0:T(8,128)(2,1)S(1)}, u32[]{:S(2)}, u32[]{:S(2)}) async-start(bf16[16,32,768]{2,1,0:T(8,128)(2,1)} %broadcast_in_dim.2), calls=%async_computation | async-start | bytes 1572864 | tf_op jit(solution)/shard_map/gather_features/all_to_all | solution.py:127
  10.0 0.0 copy-start.4
  10.7 10.0 %all-to-all-done = bf16[16,32,768]{2,1,0:T(8,128)(2,1)S(1)} async-done(((bf16[16,32,768]{2,1,0:T(8,128)(2,1)}), bf16[16,32,768]{2,1,0:T(8,128)(2,1)S(1)}, u32[]{:S(2)}, u32[]{:S(2)}) %all-to-all-start) | async-done | bytes 786464 | tf_op jit(solution)/shard_map/gather_features/all_to_all | solution.py:127
  20.7 0.0 copy-start
  20.7 1.9 %copy-done = bf16[96,128,128]{2,1,0:T(8,128)(2,1)S(1)} copy-done((bf16[96,128,128]{2,1,0:T(8,128)(2,1)S(1)}, bf16[96,128,128]{2,1,0:T(8,128)(2,1)}, u32[]{:S(2)}) %copy-start) | copy-done | bytes 3145752
  22.6 0.0 copy-start.1
  22.6 0.8 copy-done.1
  23.4 0.0 copy-start.2
  23.4 0.8 copy-done.2
  24.1 0.0 copy-start.3
  24.1 0.7 copy-done.3
  24.8 0.0 copy-start.5
  24.8 0.7 copy-done.5
  25.5 0.0 copy-start.6
  25.5 0.7 copy-done.6
  26.1 0.0 copy-start.7
  26.1 0.7 copy-done.7
  26.8 3.5 %partials.1 = bf16[32,40,128]{2,1,0:T(8,128)(2,1)S(1)} custom-call(s32[96]{0:T(128)S(1)} %copy-done.5, s32[96]{0:T(128)S(1)} %copy-done.6, s32[1]{0:T(128)S(6)} %copy.12.count_ref, s32[1,32]{1,0:T(1,128)S(1)} %copy-done.3, s32[1,32]{1,0:T(1,128)S(1)} %copy-done.7, bf16[512,768]{1,0:T(8,128)(2,1)S(1)} %bitcast.1, bf16[32,512]{1,0:T(8,128)(2,1)S(1)} %copy-done.2, ...), custom_call_target="tpu_custom_call" | custom-call | tf_op jit(solution)/shard_map/partials/pallas_call | solution.py:128
  30.3 44.7 %all_to_all.15.got_ref = bf16[32,40,128]{2,1,0:T(8,128)(2,1)S(1)} all-to-all(bf16[32,40,128]{2,1,0:T(8,128)(2,1)S(1)} %partials.1), channel_id=1, replica_groups=mesh['dom'=32,'feat'=16] {'dom'}, dimensions={0} | all-to-all | bytes 655360 | tf_op jit(solution)/shard_map/to_masters/all_to_all | solution.py:145
  75.0 1.1 %masters.1 = (bf16[32,768]{1,0:T(8,128)(2,1)}, bf16[32,40,128]{2,1,0:T(8,128)(2,1)S(1)}) custom-call(bf16[32,40,128]{2,1,0:T(8,128)(2,1)S(1)} %all_to_all.15.got_ref), custom_call_target="tpu_custom_call" | custom-call | tf_op jit(solution)/shard_map/masters/pallas_call | solution.py:146
  76.1 28.6 %all_to_all.16.got_ref = bf16[32,40,128]{2,1,0:T(8,128)(2,1)S(1)} all-to-all(bf16[32,40,128]{2,1,0:T(8,128)(2,1)S(1)} %get-tuple-element.8), channel_id=1, replica_groups=mesh['dom'=32,'feat'=16] {'dom'}, dimensions={0} | all-to-all | bytes 655360 | tf_op jit(solution)/shard_map/to_mirrors/all_to_all | solution.py:158
  104.7 0.0 copy-done.4
  104.7 1.3 %mirrors.1 = (bf16[32,4096]{1,0:T(8,128)(2,1)}, f32[32,512]{1,0:T(8,128)}) custom-call(s32[1,32]{1,0:T(1,128)S(1)} %copy-done.4, bf16[32,40,128]{2,1,0:T(8,128)(2,1)S(1)} %all_to_all.16.got_ref), custom_call_target="tpu_custom_call" | custom-call | tf_op jit(solution)/shard_map/mirrors/pallas_call | solution.py:159
Async XLA Ops:
  2.4 18.3 %all-to-all-start = ((bf16[16,32,768]{2,1,0:T(8,128)(2,1)}), bf16[16,32,768]{2,1,0:T(8,128)(2,1)S(1)}, u32[]{:S(2)}, u32[]{:S(2)}) async-start(bf16[16,32,768]{2,1,0:T(8,128)(2,1)} %broadcast_in_dim.2), calls=%async_computation | async-start | bytes 1572864 | tf_op jit(solution)/shard_map/gather_features/all_to_all | solution.py:127
  10.0 94.7 %copy-start.4 = (s32[1,32]{1,0:T(1,128)S(1)}, s32[1,32]{1,0:T(1,128)}, u32[]{:S(2)}) copy-start(s32[1,32]{1,0:T(1,128)} %owner_ref.3) | copy-start | bytes 388
  20.7 1.9 %copy-start = (bf16[96,128,128]{2,1,0:T(8,128)(2,1)S(1)}, bf16[96,128,128]{2,1,0:T(8,128)(2,1)}, u32[]{:S(2)}) copy-start(bf16[96,128,128]{2,1,0:T(8,128)(2,1)} %tiles_ref.1) | copy-start | bytes 9437188
  22.6 0.8 copy-start.1
  23.4 0.8 copy-start.2
  24.1 0.7 copy-start.3
  24.8 0.7 copy-start.5
  25.5 0.7 copy-start.6
  26.1 0.7 copy-start.7

commit v2 on v1

--- a/solution.py
+++ b/solution.py
@@ -10,25 +10,66 @@
 LANES = 128
 UNROLL = 8
 EXTRA = 8
+TILE_PARTS = 4
 VMEM_BYTES = 16 * 1024 * 1024
 
 
+def spread_kernel(source_ref, copies_ref, sems):
+    count = copies_ref.shape[0]
+    moves = [
+        pltpu.make_async_copy(source_ref, copies_ref.at[k], sems.at[k]) for k in range(count)
+    ]
+    for move in moves:
+        move.start()
+    for move in moves:
+        move.wait()
+
+
 def partial_kernel(
-    dst_ref, slot_ref, count_ref, owner_ref, local_ref,
-    piece_ref, weight_ref, agg_ref, tiles_ref,
+    dst_hbm, slot_hbm, count_ref, owner_hbm, local_hbm,
+    piece_ref, weight_hbm, agg_hbm, tiles_hbm,
     msg_ref,
-    back_ref, acc_ref, extra_ref,
+    dst_ref, slot_ref, owner_ref, local_ref, weight_ref, agg_ref, tiles_ref,
+    back_ref, acc_ref, extra_ref, sems,
 ):
     block_count, rows, _ = back_ref.shape
     peers = msg_ref.shape[0]
     tile_total = tiles_ref.shape[0]
     wide = weight_ref.shape[1] // LANES
+    pairs = [
+        (weight_hbm, weight_ref), (dst_hbm, dst_ref), (slot_hbm, slot_ref),
+        (owner_hbm, owner_ref), (local_hbm, local_ref), (agg_hbm, agg_ref),
+    ]
+    part = tile_total // TILE_PARTS
+    for k in range(TILE_PARTS):
+        pairs.append((tiles_hbm.at[pl.ds(k * part, part)], tiles_ref.at[pl.ds(k * part, part)]))
+    moves = [pltpu.make_async_copy(a, b, sems.at[k]) for k, (a, b) in enumerate(pairs)]
+    for move in moves:
+        move.start()
+    acc_ref[...] = jnp.zeros_like(acc_ref)
     piece = piece_ref[...]
+    moves[0].wait()
     back = jnp.dot(weight_ref[...], piece, preferred_element_type=jnp.float32)
     back = back.astype(jnp.bfloat16)
     for b in range(block_count):
         back_ref[b] = back[:, b * LANES : (b + 1) * LANES]
-    acc_ref[...] = jnp.zeros_like(acc_ref)
+    for move in moves[1:6]:
+        move.wait()
+    term = lax.dot_general(
+        agg_ref[...], piece, (((1,), (1,)), ((), ())), preferred_element_type=jnp.float32
+    )
+    for k in range(wide):
+        extra_ref[:, k, :] = term[:, k * LANES : (k + 1) * LANES]
+    for k in range(wide, EXTRA):
+        extra_ref[:, k, :] = jnp.zeros((peers, LANES), jnp.float32)
+
+    def number(s, carry):
+        value = local_ref[0, s].astype(jnp.float32)
+        extra_ref[owner_ref[0, s], pl.ds(wide, 1), :] = jnp.full((1, LANES), value, jnp.float32)
+        return carry
+
+    lax.fori_loop(0, peers, number, 0)
+    msg_ref[:, rows:, :] = extra_ref[...].astype(jnp.bfloat16)
     count = count_ref[0]
 
     def step(i, carry):
@@ -43,24 +84,10 @@
             acc_ref[place] += product
         return carry
 
-    lax.fori_loop(0, tile_total // UNROLL, step, 0)
-
-    term = lax.dot_general(
-        agg_ref[...], piece, (((1,), (1,)), ((), ())), preferred_element_type=jnp.float32
-    )
-    for k in range(wide):
-        extra_ref[:, k, :] = term[:, k * LANES : (k + 1) * LANES]
-    for k in range(wide, EXTRA):
-        extra_ref[:, k, :] = jnp.zeros((peers, LANES), jnp.float32)
-
-    def number(s, carry):
-        value = local_ref[0, s].astype(jnp.float32)
-        extra_ref[owner_ref[0, s], pl.ds(wide, 1), :] = jnp.full((1, LANES), value, jnp.float32)
-        return carry
-
-    lax.fori_loop(0, peers, number, 0)
+    for k in range(TILE_PARTS):
+        moves[6 + k].wait()
+        lax.fori_loop(k * part // UNROLL, (k + 1) * part // UNROLL, step, 0)
     msg_ref[:, :rows, :] = acc_ref[:peers].astype(jnp.bfloat16)
-    msg_ref[:, rows:, :] = extra_ref[...].astype(jnp.bfloat16)
 
 
 def master_kernel(wide, got_ref, nodes_ref, msg_ref):
@@ -100,6 +127,10 @@
         wgrad_ref[:, k * LANES : (k + 1) * LANES] = tail[:, k, :] + tail[:, wide + k, :]
 
 
+def in_hbm(array):
+    return pltpu.with_memory_space_constraint(array, pltpu.HBM)
+
+
 def body(
     grad_out,
     saved_agg,
@@ -120,26 +151,44 @@
     height = rows + EXTRA
     vmem = pl.BlockSpec(memory_space=pltpu.VMEM)
     smem = pl.BlockSpec(memory_space=pltpu.SMEM)
+    hbm = pl.BlockSpec(memory_space=pltpu.HBM)
     params = pltpu.CompilerParams(vmem_limit_bytes=VMEM_BYTES)
 
+    copies = pl.pallas_call(
+        spread_kernel,
+        out_shape=jax.ShapeDtypeStruct((groups, rows, columns), grad_out.dtype),
+        in_specs=[hbm],
+        out_specs=vmem,
+        scratch_shapes=[pltpu.SemaphoreType.DMA((groups,))],
+        compiler_params=params,
+        name="spread",
+    )(in_hbm(grad_out))
     with jax.named_scope("gather_features"):
-        copies = jnp.broadcast_to(grad_out[None], (groups, rows, columns))
         piece = lax.all_to_all(copies, "feat", 0, 0, tiled=True).reshape(features, columns)
     message = pl.pallas_call(
         partial_kernel,
         out_shape=jax.ShapeDtypeStruct((peers, height, LANES), jnp.bfloat16),
-        in_specs=[smem] * 5 + [vmem] * 4,
+        in_specs=[hbm] * 2 + [smem] + [hbm] * 2 + [vmem] + [hbm] * 3,
         out_specs=vmem,
         scratch_shapes=[
+            pltpu.SMEM(tile_dst.shape, jnp.int32),
+            pltpu.SMEM(tile_slot.shape, jnp.int32),
+            pltpu.SMEM(mirror_owner.shape, jnp.int32),
+            pltpu.SMEM(mirror_local.shape, jnp.int32),
+            pltpu.VMEM(weight.shape, jnp.bfloat16),
+            pltpu.VMEM(saved_agg.shape, jnp.bfloat16),
+            pltpu.VMEM(tile_values.shape, jnp.bfloat16),
             pltpu.VMEM((block_count, rows, LANES), jnp.bfloat16),
             pltpu.VMEM((peers + 1, rows, LANES), jnp.float32),
             pltpu.VMEM((peers, EXTRA, LANES), jnp.float32),
+            pltpu.SemaphoreType.DMA((6 + TILE_PARTS,)),
         ],
         compiler_params=params,
         name="partials",
     )(
-        tile_dst, tile_slot, tile_count, mirror_owner, mirror_local,
-        piece, weight, saved_agg, tile_values,
+        in_hbm(tile_dst), in_hbm(tile_slot), tile_count, in_hbm(mirror_owner), in_hbm(mirror_local),
+        piece,
+        *map(in_hbm, (weight, saved_agg, tile_values)),
     )
     with jax.named_scope("to_masters"):
         got = lax.all_to_all(message, "dom", 0, 0, tiled=True)

time: 107 us -> 102 us (0.953)
  local copies, waits for them, and re-layouts: 7.84 us -> 0.01 us
  Pallas kernels: 5.95 us -> 9.28 us
    unnamed x16 -> x2, local copies, waits for them, and re-layouts: 6.07 us -> 0.01 us
    pallas_call x0 -> x1, Pallas kernels: none -> 2.84 us  [body(): pl.pallas_call(spread_kernel, out_shape=jax.ShapeDtypeStruct((groups, row...]
    broadcast_in_dim x1 -> x0, local copies, waits for them, and re-layouts: 1.77 us -> none  [body(): copies = jnp.broadcast_to(grad_out[None], (groups, rows, columns))]
where the time goes in v2:
time: 102 us
  blocking collectives  73.3 us (72%)
  waiting for transfers between devices  10 us (10%)
  Pallas kernels  9.28 us (9%)
  starting transfers between devices  7.6 us (7%)
  between operations  1.32 us (1%)
    all_to_all x1, blocking collectives, body(): got = lax.all_to_all(message, 'dom', 0, 0, tiled=True)  44.7 us
    all_to_all x1, blocking collectives, body(): back = lax.all_to_all(answer, 'dom', 0, 0, tiled=True)  28.6 us
    all_to_all x1, waiting for transfers between devices, body(): lax.all_to_all(copies, 'feat', 0, 0, tiled=True).reshape(features, columns)  10 us
    all_to_all x1, starting transfers between devices, body(): lax.all_to_all(copies, 'feat', 0, 0, tiled=True).reshape(features, columns)  7.6 us
    pallas_call x1, Pallas kernels, body(): pl.pallas_call(partial_kernel, out_shape=jax.ShapeDtypeStruct((peers, hei...  4.04 us
    pallas_call x1, Pallas kernels, body(): pl.pallas_call(spread_kernel, out_shape=jax.ShapeDtypeStruct((groups, row...  2.84 us
  transfers between devices with their start and end apart: 1, of which 1 were waited for; matrix products, arithmetic and copies ran while one was open for 0% of the time, Pallas kernels for 0%

profile of v2, /device:TPU:1, one launch (start us, length us, event | category | flops | bytes accessed | tf_op | source)
XLA Modules:
  0.0 101.5 jit_solution(3720436426086394655)
XLA Ops:
  0.6 2.8 %spread.1 = bf16[16,32,768]{2,1,0:T(8,128)(2,1)} custom-call(bf16[32,768]{1,0:T(8,128)(2,1)} %source_ref.1), custom_call_target="tpu_custom_call" | custom-call | tf_op jit(solution)/shard_map/spread/pallas_call | solution.py:157
  3.5 7.6 %all-to-all-start = ((bf16[16,32,768]{2,1,0:T(8,128)(2,1)}), bf16[16,32,768]{2,1,0:T(8,128)(2,1)S(1)}, u32[]{:S(2)}, u32[]{:S(2)}) async-start(bf16[16,32,768]{2,1,0:T(8,128)(2,1)} %spread.1), calls=%async_computation | async-start | bytes 1572864 | tf_op jit(solution)/shard_map/gather_features/all_to_all | solution.py:167
  11.1 0.0 copy-start
  11.8 10.0 %all-to-all-done = bf16[16,32,768]{2,1,0:T(8,128)(2,1)S(1)} async-done(((bf16[16,32,768]{2,1,0:T(8,128)(2,1)}), bf16[16,32,768]{2,1,0:T(8,128)(2,1)S(1)}, u32[]{:S(2)}, u32[]{:S(2)}) %all-to-all-start) | async-done | bytes 786464 | tf_op jit(solution)/shard_map/gather_features/all_to_all | solution.py:167
  21.8 4.0 %partials.1 = bf16[32,40,128]{2,1,0:T(8,128)(2,1)S(1)} custom-call(s32[96]{0:T(128)} %dst_hbm.1, s32[96]{0:T(128)} %slot_hbm.1, s32[1]{0:T(128)S(6)} %copy.12.count_ref, s32[1,32]{1,0:T(1,128)} %owner_ref.1, s32[1,32]{1,0:T(1,128)} %local_hbm.1, bf16[512,768]{1,0:T(8,128)(2,1)S(1)} %bitcast.1, bf16[32,512]{1,0:T(8,128)(2,1)} %weight_hbm.1, ...), custom_call_target="tpu_custom_call" | custom-call | tf_op jit(solution)/shard_map/partials/pallas_call | solution.py:168
  25.8 44.7 %all_to_all.15.got_ref = bf16[32,40,128]{2,1,0:T(8,128)(2,1)S(1)} all-to-all(bf16[32,40,128]{2,1,0:T(8,128)(2,1)S(1)} %partials.1), channel_id=1, replica_groups=mesh['dom'=32,'feat'=16] {'dom'}, dimensions={0} | all-to-all | bytes 655360 | tf_op jit(solution)/shard_map/to_masters/all_to_all | solution.py:194
  70.5 1.1 %masters.1 = (bf16[32,768]{1,0:T(8,128)(2,1)}, bf16[32,40,128]{2,1,0:T(8,128)(2,1)S(1)}) custom-call(bf16[32,40,128]{2,1,0:T(8,128)(2,1)S(1)} %all_to_all.15.got_ref), custom_call_target="tpu_custom_call" | custom-call | tf_op jit(solution)/shard_map/masters/pallas_call | solution.py:195
  71.6 28.6 %all_to_all.16.got_ref = bf16[32,40,128]{2,1,0:T(8,128)(2,1)S(1)} all-to-all(bf16[32,40,128]{2,1,0:T(8,128)(2,1)S(1)} %get-tuple-element.8), channel_id=1, replica_groups=mesh['dom'=32,'feat'=16] {'dom'}, dimensions={0} | all-to-all | bytes 655360 | tf_op jit(solution)/shard_map/to_mirrors/all_to_all | solution.py:207
  100.2 0.0 copy-done
  100.2 1.3 %mirrors.1 = (bf16[32,4096]{1,0:T(8,128)(2,1)}, f32[32,512]{1,0:T(8,128)}) custom-call(s32[1,32]{1,0:T(1,128)S(1)} %copy-done, bf16[32,40,128]{2,1,0:T(8,128)(2,1)S(1)} %all_to_all.16.got_ref), custom_call_target="tpu_custom_call" | custom-call | tf_op jit(solution)/shard_map/mirrors/pallas_call | solution.py:208
Async XLA Ops:
  3.5 18.3 %all-to-all-start = ((bf16[16,32,768]{2,1,0:T(8,128)(2,1)}), bf16[16,32,768]{2,1,0:T(8,128)(2,1)S(1)}, u32[]{:S(2)}, u32[]{:S(2)}) async-start(bf16[16,32,768]{2,1,0:T(8,128)(2,1)} %spread.1), calls=%async_computation | async-start | bytes 1572864 | tf_op jit(solution)/shard_map/gather_features/all_to_all | solution.py:167
  11.1 89.1 %copy-start = (s32[1,32]{1,0:T(1,128)S(1)}, s32[1,32]{1,0:T(1,128)}, u32[]{:S(2)}) copy-start(s32[1,32]{1,0:T(1,128)} %owner_ref.1) | copy-start | bytes 388

commit v3 on v2

v3 whole, which is shorter than its diff:
```python
import functools

import jax
import jax.numpy as jnp
from jax import lax
from jax.experimental import pallas as pl
from jax.experimental.pallas import tpu as pltpu
from jax.sharding import PartitionSpec as P

LANES = 128
GROUP = 96
EXTRA = 8
VMEM_BYTES = 16 * 1024 * 1024


def spread_kernel(source_hbm, copies_ref, source_ref, sem):
    move = pltpu.make_async_copy(source_hbm, source_ref, sem.at[0])
    move.start()
    move.wait()
    value = source_ref[...]
    for k in range(copies_ref.shape[0]):
        copies_ref[k] = value


def prefetch_kernel(weight_hbm, agg_hbm, tiles_hbm, weight_ref, agg_ref, tiles_ref, sems):
    pairs = ((weight_hbm, weight_ref), (agg_hbm, agg_ref), (tiles_hbm, tiles_ref))
    moves = [pltpu.make_async_copy(a, b, sems.at[k]) for k, (a, b) in enumerate(pairs)]
    for move in moves:
        move.start()
    for move in moves:
        move.wait()


def partial_kernel(
    dst_hbm, slot_hbm, count_ref, owner_hbm, local_hbm,
    piece_ref, weight_ref, agg_ref, tiles_ref,
    msg_ref,
    dst_ref, slot_ref, owner_ref, local_ref, back_ref, acc_ref, extra_ref, sems,
):
    block_count, rows, _ = back_ref.shape
    peers = msg_ref.shape[0]
    tile_total = tiles_ref.shape[0]
    wide = weight_ref.shape[1] // LANES
    pairs = (
        (dst_hbm, dst_ref), (slot_hbm, slot_ref), (owner_hbm, owner_ref), (local_hbm, local_ref),
    )
    moves = [pltpu.make_async_copy(a, b, sems.at[k]) for k, (a, b) in enumerate(pairs)]
    for move in moves:
        move.start()
    acc_ref[...] = jnp.zeros_like(acc_ref)
    piece = piece_ref[...]
    back = jnp.dot(weight_ref[...], piece, preferred_element_type=jnp.float32)
    back = back.astype(jnp.bfloat16)
    for b in range(block_count):
        back_ref[b] = back[:, b * LANES : (b + 1) * LANES]
    term = lax.dot_general(
        agg_ref[...], piece, (((1,), (1,)), ((), ())), preferred_element_type=jnp.float32
    )
    for k in range(wide):
        extra_ref[:, k, :] = term[:, k * LANES : (k + 1) * LANES]
    for k in range(wide, EXTRA):
        extra_ref[:, k, :] = jnp.zeros((peers, LANES), jnp.float32)
    for move in moves:
        move.wait()
    for s in range(peers):
        value = local_ref[0, s].astype(jnp.float32)
        extra_ref[owner_ref[0, s], pl.ds(wide, 1), :] = jnp.full((1, LANES), value, jnp.float32)
    msg_ref[:, rows:, :] = extra_ref[...].astype(jnp.bfloat16)
    count = count_ref[0]
    for start in range(0, tile_total, GROUP):
        products, places = [], []
        for t in range(start, min(start + GROUP, tile_total)):
            products.append(
                jnp.dot(back_ref[dst_ref[t]], tiles_ref[t], preferred_element_type=jnp.float32)
            )
            places.append(jnp.where(t < count, owner_ref[0, slot_ref[t]], peers))
        for place, product in zip(places, products):
            acc_ref[place] += product
    msg_ref[:, :rows, :] = acc_ref[:peers].astype(jnp.bfloat16)


def master_kernel(wide, got_ref, nodes_ref, msg_ref):
    peers, height, _ = got_ref.shape
    rows, columns = nodes_ref.shape
    block_count = columns // LANES
    tail = got_ref[:, rows:, :].astype(jnp.float32)
    numbers = [tail[p, wide : wide + 1, :] for p in range(peers)]
    sums = [jnp.zeros((rows, LANES), jnp.float32) for _ in range(block_count)]
    for p in range(peers):
        part = got_ref[p, :rows, :].astype(jnp.float32)
        for b in range(block_count):
            sums[b] = sums[b] + jnp.where(numbers[p] == float(b), part, 0.0)
    for b in range(block_count):
        nodes_ref[:, b * LANES : (b + 1) * LANES] = sums[b].astype(jnp.bfloat16)
    for p in range(peers):
        pick = sums[0]
        for b in range(1, block_count):
            pick = jnp.where(numbers[p] == float(b), sums[b], pick)
        msg_ref[p, :rows, :] = pick.astype(jnp.bfloat16)
    total = jnp.sum(tail, axis=0)
    high = total[:wide].astype(jnp.bfloat16)
    low = (total[:wide] - high.astype(jnp.float32)).astype(jnp.bfloat16)
    both = jnp.concatenate([high.astype(jnp.float32), low.astype(jnp.float32)], axis=0)
    both = both.astype(jnp.bfloat16)
    for p in range(peers):
        msg_ref[p, rows:, :] = both


def mirror_kernel(
    wide, owner_hbm, got_ref, kept_ref, mirrors_hbm, wgrad_hbm, nodes_hbm,
    owner_ref, wgrad_ref, sems,
):
    peers = got_ref.shape[0]
    rows = wgrad_ref.shape[0]
    first = pltpu.make_async_copy(owner_hbm, owner_ref, sems.at[0])
    first.start()
    moves = [pltpu.make_async_copy(kept_ref, nodes_hbm, sems.at[1])]
    moves[0].start()
    tail = got_ref[:, rows:, :].astype(jnp.float32)
    for k in range(wide):
        wgrad_ref[:, k * LANES : (k + 1) * LANES] = tail[:, k, :] + tail[:, wide + k, :]
    moves.append(pltpu.make_async_copy(wgrad_ref, wgrad_hbm, sems.at[2]))
    moves[1].start()
    first.wait()
    for s in range(peers):
        move = pltpu.make_async_copy(
            got_ref.at[owner_ref[0, s], pl.ds(0, rows), :],
            mirrors_hbm.at[:, pl.ds(s * LANES, LANES)],
            sems.at[3 + s],
        )
        move.start()
        moves.append(move)
    for move in moves:
        move.wait()


def in_hbm(array):
    return pltpu.with_memory_space_constraint(array, pltpu.HBM)


def body(
    grad_out,
    saved_agg,
    weight,
    tile_values,
    tile_dst,
    tile_slot,
    tile_count,
    mirror_owner,
    mirror_local,
):
    rows, columns = grad_out.shape
    block_count = columns // LANES
    peers = mirror_owner.shape[1]
    features = weight.shape[1]
    wide = features // LANES
    groups = features // rows
    height = rows + EXTRA
    vmem = pl.BlockSpec(memory_space=pltpu.VMEM)
    smem = pl.BlockSpec(memory_space=pltpu.SMEM)
    hbm = pl.BlockSpec(memory_space=pltpu.HBM)
    params = pltpu.CompilerParams(vmem_limit_bytes=VMEM_BYTES)

    copies = pl.pallas_call(
        spread_kernel,
        out_shape=pltpu.VMEM((groups, rows, columns), grad_out.dtype),
        in_specs=[hbm],
        out_specs=vmem,
        scratch_shapes=[pltpu.VMEM(grad_out.shape, grad_out.dtype), pltpu.SemaphoreType.DMA((1,))],
        compiler_params=params,
        name="spread",
    )(in_hbm(grad_out))
    with jax.named_scope("gather_features"):
        piece = lax.all_to_all(copies, "feat", 0, 0, tiled=True).reshape(features, columns)
    operands = (weight, saved_agg, tile_values)
    near = pl.pallas_call(
        prefetch_kernel,
        out_shape=tuple(pltpu.VMEM(x.shape, x.dtype) for x in operands),
        in_specs=[hbm] * 3,
        out_specs=(vmem,) * 3,
        scratch_shapes=[pltpu.SemaphoreType.DMA((3,))],
        compiler_params=params,
        cost_estimate=pl.CostEstimate(
            flops=0, transcendentals=0, bytes_accessed=2 * sum(x.size * 2 for x in operands)
        ),
        name="prefetch",
    )(*map(in_hbm, operands))
    message = pl.pallas_call(
        partial_kernel,
        out_shape=pltpu.VMEM((peers, height, LANES), jnp.bfloat16),
        in_specs=[hbm] * 2 + [smem] + [hbm] * 2 + [vmem] * 4,
        out_specs=vmem,
        scratch_shapes=[
            pltpu.SMEM(tile_dst.shape, jnp.int32),
            pltpu.SMEM(tile_slot.shape, jnp.int32),
            pltpu.SMEM(mirror_owner.shape, jnp.int32),
            pltpu.SMEM(mirror_local.shape, jnp.int32),
            pltpu.VMEM((block_count, rows, LANES), jnp.bfloat16),
            pltpu.VMEM((peers + 1, rows, LANES), jnp.float32),
            pltpu.VMEM((peers, EXTRA, LANES), jnp.float32),
            pltpu.SemaphoreType.DMA((4,)),
        ],
        compiler_params=params,
        name="partials",
    )(
        in_hbm(tile_dst), in_hbm(tile_slot), tile_count, in_hbm(mirror_owner), in_hbm(mirror_local),
        piece, *near,
    )
    with jax.named_scope("to_masters"):
        got = lax.all_to_all(message, "dom", 0, 0, tiled=True)
    kept, answer = pl.pallas_call(
        functools.partial(master_kernel, wide),
        out_shape=(
            pltpu.VMEM((rows, columns), jnp.bfloat16),
            pltpu.VMEM((peers, height, LANES), jnp.bfloat16),
        ),
        in_specs=[vmem],
        out_specs=(vmem, vmem),
        compiler_params=params,
        name="masters",
    )(got)
    with jax.named_scope("to_mirrors"):
        back = lax.all_to_all(answer, "dom", 0, 0, tiled=True)
    grad_mirrors, weight_grad, grad_nodes = pl.pallas_call(
        functools.partial(mirror_kernel, wide),
        out_shape=(
            pltpu.HBM((rows, peers * LANES), jnp.bfloat16),
            pltpu.HBM((rows, features), jnp.float32),
            pltpu.HBM((rows, columns), jnp.bfloat16),
        ),
        in_specs=[hbm, vmem, vmem],
        out_specs=(hbm, hbm, hbm),
        scratch_shapes=[
            pltpu.SMEM(mirror_owner.shape, jnp.int32),
            pltpu.VMEM((rows, features), jnp.float32),
            pltpu.SemaphoreType.DMA((3 + peers,)),
        ],
        compiler_params=params,
        name="mirrors",
    )(in_hbm(mirror_owner), back, kept)
    return (grad_nodes, grad_mirrors, weight_grad)


def solution(mesh):
    in_specs = (
        P("feat", "dom"),
        P("feat", "dom"),
        P("feat", None),
        P("dom", None, None),
        P("dom"),
        P("dom"),
        P("dom"),
        P("dom", None),
        P("dom", None),
    )
    out_specs = (P("feat", "dom"), P("feat", "dom"), P("feat", None))
    return jax.shard_map(body, mesh=mesh, in_specs=in_specs, out_specs=out_specs, check_vma=False)
```

time: 102 us -> 100 us (0.980)
  waiting for transfers between devices: 10 us -> 8.12 us
    all_to_all x1, waiting for transfers between devices: 10 us -> 8.12 us  [body(): lax.all_to_all(copies, 'feat', 0, 0, tiled=True).reshape(features, columns)]
    pallas_call x4 -> x5, Pallas kernels: 9.28 us -> 9.3 us  [the longest x1 3.27 us: body(): pl.pallas_call(partial_kernel, out_shape=pltpu.VMEM((peers, height, LANES...]
  transfers between devices with their start and end apart: 1 -> 1, of which waited for: 1 -> 1; matrix products, arithmetic and copies ran while one was open for 0% -> 0% of each run, Pallas kernels for 0% -> 2%
where the time goes in v3:
time: 100 us; the launch traced here: 99.7 us
  blocking collectives  73.3 us (73%)
  Pallas kernels  9.3 us (9%)
  waiting for transfers between devices  8.12 us (8%)
  starting transfers between devices  7.64 us (8%)
  between operations  1.31 us (1%)
    all_to_all x1, blocking collectives, body(): got = lax.all_to_all(message, 'dom', 0, 0, tiled=True)  44.7 us
    all_to_all x1, blocking collectives, body(): back = lax.all_to_all(answer, 'dom', 0, 0, tiled=True)  28.6 us
    all_to_all x1, waiting for transfers between devices, body(): lax.all_to_all(copies, 'feat', 0, 0, tiled=True).reshape(features, columns)  8.12 us
    all_to_all x1, starting transfers between devices, body(): lax.all_to_all(copies, 'feat', 0, 0, tiled=True).reshape(features, columns)  7.64 us
    pallas_call x1, Pallas kernels, body(): pl.pallas_call(partial_kernel, out_shape=pltpu.VMEM((peers, height, LANES...  3.27 us
  transfers between devices with their start and end apart: 1, of which 1 were waited for; matrix products, arithmetic and copies ran while one was open for 0% of the time, Pallas kernels for 2%

profile of v3, /device:TPU:1, one launch (start us, length us, event | category | flops | bytes accessed | tf_op | source)
XLA Modules:
  0.0 99.7 jit_solution(17459145359020789901)
XLA Ops:
  0.6 1.8 %spread.1 = bf16[16,32,768]{2,1,0:T(8,128)(2,1)} custom-call(bf16[32,768]{1,0:T(8,128)(2,1)} %source_hbm.1), custom_call_target="tpu_custom_call" | custom-call | tf_op jit(solution)/shard_map/spread/pallas_call | solution.py:164
  2.4 7.6 %all-to-all-start = ((bf16[16,32,768]{2,1,0:T(8,128)(2,1)}), bf16[16,32,768]{2,1,0:T(8,128)(2,1)}, u32[]{:S(2)}, u32[]{:S(2)}) async-start(bf16[16,32,768]{2,1,0:T(8,128)(2,1)} %spread.1), calls=%async_computation | async-start | bytes 1572864 | tf_op jit(solution)/shard_map/gather_features/all_to_all | solution.py:174
  10.7 2.0 %prefetch.1 = (bf16[32,512]{1,0:T(8,128)(2,1)S(1)}, bf16[32,768]{1,0:T(8,128)(2,1)S(1)}, bf16[96,128,128]{2,1,0:T(8,128)(2,1)S(1)}) custom-call(bf16[32,512]{1,0:T(8,128)(2,1)} %weight_hbm.1, bf16[32,768]{1,0:T(8,128)(2,1)} %agg_hbm.1, bf16[96,128,128]{2,1,0:T(8,128)(2,1)} %tiles_hbm.1), custom_call_target="tpu_custom_call" | custom-call | bytes 6455296 | tf_op jit(solution)/shard_map/prefetch/pallas_call | solution.py:176
  12.7 8.1 %all-to-all-done = bf16[16,32,768]{2,1,0:T(8,128)(2,1)} async-done(((bf16[16,32,768]{2,1,0:T(8,128)(2,1)}), bf16[16,32,768]{2,1,0:T(8,128)(2,1)}, u32[]{:S(2)}, u32[]{:S(2)}) %all-to-all-start) | async-done | bytes 786464 | tf_op jit(solution)/shard_map/gather_features/all_to_all | solution.py:174
  20.8 3.3 %partials.1 = bf16[32,40,128]{2,1,0:T(8,128)(2,1)S(1)} custom-call(s32[96]{0:T(128)} %dst_hbm.1, s32[96]{0:T(128)} %slot_hbm.1, s32[1]{0:T(128)S(6)} %copy.12.count_ref, s32[1,32]{1,0:T(1,128)} %owner_hbm.3, s32[1,32]{1,0:T(1,128)} %local_hbm.1, bf16[512,768]{1,0:T(8,128)(2,1)} %bitcast.piece_ref, bf16[32,512]{1,0:T(8,128)(2,1)S(1)} %get-tuple-element.11.weight_ref, ...), custom_call_target="tpu_custom_call" | custom-call | tf_op jit(solution)/shard_map/partials/pallas_call | solution.py:188
  24.1 44.7 %all_to_all.15.got_ref = bf16[32,40,128]{2,1,0:T(8,128)(2,1)S(1)} all-to-all(bf16[32,40,128]{2,1,0:T(8,128)(2,1)S(1)} %partials.1), channel_id=1, replica_groups=mesh['dom'=32,'feat'=16] {'dom'}, dimensions={0} | all-to-all | bytes 655360 | tf_op jit(solution)/shard_map/to_masters/all_to_all | solution.py:210
  68.8 0.6 masters.1
  69.4 28.6 %all_to_all.16.got_ref = bf16[32,40,128]{2,1,0:T(8,128)(2,1)S(1)} all-to-all(bf16[32,40,128]{2,1,0:T(8,128)(2,1)S(1)} %get-tuple-element.14), channel_id=1, replica_groups=mesh['dom'=32,'feat'=16] {'dom'}, dimensions={0} | all-to-all | bytes 655360 | tf_op jit(solution)/shard_map/to_mirrors/all_to_all | solution.py:223
  98.0 1.7 %mirrors.1 = (bf16[32,4096]{1,0:T(8,128)(2,1)}, f32[32,512]{1,0:T(8,128)}, bf16[32,768]{1,0:T(8,128)(2,1)}) custom-call(s32[1,32]{1,0:T(1,128)} %owner_hbm.3, bf16[32,40,128]{2,1,0:T(8,128)(2,1)S(1)} %all_to_all.16.got_ref, bf16[32,768]{1,0:T(8,128)(2,1)S(1)} %get-tuple-element.15.kept_ref), custom_call_target="tpu_custom_call" | custom-call | tf_op jit(solution)/shard_map/mirrors/pallas_call | solution.py:224
Async XLA Ops:
  2.4 18.4 %all-to-all-start = ((bf16[16,32,768]{2,1,0:T(8,128)(2,1)}), bf16[16,32,768]{2,1,0:T(8,128)(2,1)}, u32[]{:S(2)}, u32[]{:S(2)}) async-start(bf16[16,32,768]{2,1,0:T(8,128)(2,1)} %spread.1), calls=%async_computation | async-start | bytes 1572864 | tf_op jit(solution)/shard_map/gather_features/all_to_all | solution.py:174

commit v4 on v3

--- a/solution.py
+++ b/solution.py
@@ -11,6 +11,16 @@
 GROUP = 96
 EXTRA = 8
 VMEM_BYTES = 16 * 1024 * 1024
+DOM_FIRST = 17
+FEAT_FIRST = 10
+
+
+def order_of(first, count):
+    return [first] + [k for k in range(count) if k != first]
+
+
+def place_of(index, first):
+    return jnp.where(index == first, 0, index + (index < first).astype(jnp.int32))
 
 
 def spread_kernel(source_hbm, copies_ref, source_ref, sem):
@@ -35,7 +45,7 @@
     dst_hbm, slot_hbm, count_ref, owner_hbm, local_hbm,
     piece_ref, weight_ref, agg_ref, tiles_ref,
     msg_ref,
-    dst_ref, slot_ref, owner_ref, local_ref, back_ref, acc_ref, extra_ref, sems,
+    dst_ref, slot_ref, owner_ref, local_ref, place_ref, back_ref, acc_ref, extra_ref, sems,
 ):
     block_count, rows, _ = back_ref.shape
     peers = msg_ref.shape[0]
@@ -48,7 +58,13 @@
     for move in moves:
         move.start()
     acc_ref[...] = jnp.zeros_like(acc_ref)
-    piece = piece_ref[...]
+    groups = piece_ref.shape[0]
+    piece = jnp.concatenate(
+        [piece_ref[k] for k in range(1, FEAT_FIRST + 1)]
+        + [piece_ref[0]]
+        + [piece_ref[k] for k in range(FEAT_FIRST + 1, groups)],
+        axis=0,
+    )
     back = jnp.dot(weight_ref[...], piece, preferred_element_type=jnp.float32)
     back = back.astype(jnp.bfloat16)
     for b in range(block_count):
@@ -64,7 +80,9 @@
         move.wait()
     for s in range(peers):
         value = local_ref[0, s].astype(jnp.float32)
-        extra_ref[owner_ref[0, s], pl.ds(wide, 1), :] = jnp.full((1, LANES), value, jnp.float32)
+        place = place_of(owner_ref[0, s], DOM_FIRST)
+        place_ref[s] = place
+        extra_ref[place, pl.ds(wide, 1), :] = jnp.full((1, LANES), value, jnp.float32)
     msg_ref[:, rows:, :] = extra_ref[...].astype(jnp.bfloat16)
     count = count_ref[0]
     for start in range(0, tile_total, GROUP):
@@ -73,7 +91,7 @@
             products.append(
                 jnp.dot(back_ref[dst_ref[t]], tiles_ref[t], preferred_element_type=jnp.float32)
             )
-            places.append(jnp.where(t < count, owner_ref[0, slot_ref[t]], peers))
+            places.append(jnp.where(t < count, place_ref[slot_ref[t]], peers))
         for place, product in zip(places, products):
             acc_ref[place] += product
     msg_ref[:, :rows, :] = acc_ref[:peers].astype(jnp.bfloat16)
@@ -124,7 +142,7 @@
     first.wait()
     for s in range(peers):
         move = pltpu.make_async_copy(
-            got_ref.at[owner_ref[0, s], pl.ds(0, rows), :],
+            got_ref.at[place_of(owner_ref[0, s], DOM_FIRST), pl.ds(0, rows), :],
             mirrors_hbm.at[:, pl.ds(s * LANES, LANES)],
             sems.at[3 + s],
         )
@@ -156,6 +174,7 @@
     wide = features // LANES
     groups = features // rows
     height = rows + EXTRA
+    dom_groups = [order_of(DOM_FIRST, peers)]
     vmem = pl.BlockSpec(memory_space=pltpu.VMEM)
     smem = pl.BlockSpec(memory_space=pltpu.SMEM)
     hbm = pl.BlockSpec(memory_space=pltpu.HBM)
@@ -171,7 +190,9 @@
         name="spread",
     )(in_hbm(grad_out))
     with jax.named_scope("gather_features"):
-        piece = lax.all_to_all(copies, "feat", 0, 0, tiled=True).reshape(features, columns)
+        piece = lax.all_to_all(
+            copies, "feat", 0, 0, tiled=True, axis_index_groups=[order_of(FEAT_FIRST, groups)]
+        )
     operands = (weight, saved_agg, tile_values)
     near = pl.pallas_call(
         prefetch_kernel,
@@ -195,6 +216,7 @@
             pltpu.SMEM(tile_slot.shape, jnp.int32),
             pltpu.SMEM(mirror_owner.shape, jnp.int32),
             pltpu.SMEM(mirror_local.shape, jnp.int32),
+            pltpu.SMEM((peers,), jnp.int32),
             pltpu.VMEM((block_count, rows, LANES), jnp.bfloat16),
             pltpu.VMEM((peers + 1, rows, LANES), jnp.float32),
             pltpu.VMEM((peers, EXTRA, LANES), jnp.float32),
@@ -207,7 +229,7 @@
         piece, *near,
     )
     with jax.named_scope("to_masters"):
-        got = lax.all_to_all(message, "dom", 0, 0, tiled=True)
+        got = lax.all_to_all(message, "dom", 0, 0, tiled=True, axis_index_groups=dom_groups)
     kept, answer = pl.pallas_call(
         functools.partial(master_kernel, wide),
         out_shape=(
@@ -220,7 +242,7 @@
         name="masters",
     )(got)
     with jax.named_scope("to_mirrors"):
-        back = lax.all_to_all(answer, "dom", 0, 0, tiled=True)
+        back = lax.all_to_all(answer, "dom", 0, 0, tiled=True, axis_index_groups=dom_groups)
     grad_mirrors, weight_grad, grad_nodes = pl.pallas_call(
         functools.partial(mirror_kernel, wide),
         out_shape=(

time: 100 us -> 90 us (0.900)
  blocking collectives: 73.3 us -> 65.5 us
  waiting for transfers between devices: 8.12 us -> 3.39 us
  starting transfers between devices: 7.64 us -> 10.2 us
    all_to_all x2, blocking collectives: 73.3 us -> 65.5 us  [the longest x1 38.1 us: body(): lax.all_to_all(message, 'dom', 0, 0, tiled=True, axis_index_groups=dom_gr...]
    all_to_all x1, waiting for transfers between devices: 8.12 us -> 3.39 us  [body(): lax.all_to_all(copies, 'feat', 0, 0, tiled=True, axis_index_groups=[order...]
    all_to_all x1, starting transfers between devices: 7.64 us -> 10.2 us  [body(): lax.all_to_all(copies, 'feat', 0, 0, tiled=True, axis_index_groups=[order...]
where the time goes in v4:
time: 90 us; the launch traced here: 89.6 us
  blocking collectives  65.5 us (73%)
  starting transfers between devices  10.2 us (11%)
  Pallas kernels  9.26 us (10%)
  waiting for transfers between devices  3.39 us (4%)
  between operations  1.31 us (1%)
    all_to_all x1, blocking collectives, body(): lax.all_to_all(message, 'dom', 0, 0, tiled=True, axis_index_groups=dom_gr...  38.1 us
    all_to_all x1, blocking collectives, body(): lax.all_to_all(answer, 'dom', 0, 0, tiled=True, axis_index_groups=dom_gro...  27.4 us
    all_to_all x1, starting transfers between devices, body(): lax.all_to_all(copies, 'feat', 0, 0, tiled=True, axis_index_groups=[order...  10.2 us
    all_to_all x1, waiting for transfers between devices, body(): lax.all_to_all(copies, 'feat', 0, 0, tiled=True, axis_index_groups=[order...  3.39 us
    pallas_call x1, Pallas kernels, body(): pl.pallas_call(partial_kernel, out_shape=pltpu.VMEM((peers, height, LANES...  3.22 us
    pallas_call x1, Pallas kernels, body(): pl.pallas_call(prefetch_kernel, out_shape=tuple((pltpu.VMEM(x.shape, x.dt...  1.97 us
  transfers between devices with their start and end apart: 1, of which 1 were waited for; matrix products, arithmetic and copies ran while one was open for 0% of the time, Pallas kernels for 2%

profile of v4, /device:TPU:1, one launch (start us, length us, event | category | flops | bytes accessed | tf_op | source)
XLA Modules:
  0.0 89.6 jit_solution(18249390004728171459)
XLA Ops:
  0.6 1.8 %spread.1 = bf16[16,32,768]{2,1,0:T(8,128)(2,1)} custom-call(bf16[32,768]{1,0:T(8,128)(2,1)} %source_hbm.1), custom_call_target="tpu_custom_call" | custom-call | tf_op jit(solution)/shard_map/spread/pallas_call | solution.py:183
  2.4 10.2 %all-to-all-start = ((bf16[16,32,768]{2,1,0:T(8,128)(2,1)}), bf16[16,32,768]{2,1,0:T(8,128)(2,1)}, u32[]{:S(2)}, u32[]{:S(2)}) async-start(bf16[16,32,768]{2,1,0:T(8,128)(2,1)} %spread.1), calls=%async_computation | async-start | bytes 1572864 | tf_op jit(solution)/shard_map/gather_features/all_to_all | solution.py:193
  13.3 2.0 %prefetch.1 = (bf16[32,512]{1,0:T(8,128)(2,1)S(1)}, bf16[32,768]{1,0:T(8,128)(2,1)S(1)}, bf16[96,128,128]{2,1,0:T(8,128)(2,1)S(1)}) custom-call(bf16[32,512]{1,0:T(8,128)(2,1)} %weight_hbm.1, bf16[32,768]{1,0:T(8,128)(2,1)} %agg_hbm.1, bf16[96,128,128]{2,1,0:T(8,128)(2,1)} %tiles_hbm.1), custom_call_target="tpu_custom_call" | custom-call | bytes 6455296 | tf_op jit(solution)/shard_map/prefetch/pallas_call | solution.py:197
  15.3 3.4 %all-to-all-done.piece_ref = bf16[16,32,768]{2,1,0:T(8,128)(2,1)} async-done(((bf16[16,32,768]{2,1,0:T(8,128)(2,1)}), bf16[16,32,768]{2,1,0:T(8,128)(2,1)}, u32[]{:S(2)}, u32[]{:S(2)}) %all-to-all-start) | async-done | bytes 786464 | tf_op jit(solution)/shard_map/gather_features/all_to_all | solution.py:193
  18.7 3.2 %partials.1 = bf16[32,40,128]{2,1,0:T(8,128)(2,1)S(1)} custom-call(s32[96]{0:T(128)} %dst_hbm.1, s32[96]{0:T(128)} %slot_hbm.1, s32[1]{0:T(128)S(6)} %copy.12.count_ref, s32[1,32]{1,0:T(1,128)} %owner_hbm.3, s32[1,32]{1,0:T(1,128)} %local_hbm.1, bf16[16,32,768]{2,1,0:T(8,128)(2,1)} %all-to-all-done.piece_ref, ...), custom_call_target="tpu_custom_call" | custom-call | tf_op jit(solution)/shard_map/partials/pallas_call | solution.py:209
  21.9 38.1 %all_to_all.15.got_ref = bf16[32,40,128]{2,1,0:T(8,128)(2,1)S(1)} all-to-all(bf16[32,40,128]{2,1,0:T(8,128)(2,1)S(1)} %partials.1), channel_id=1, replica_groups={{272,0,16,32,48,64,80,96,112,128,144,160,176,192,208,224,240,256,288,30..., dimensions={0} | all-to-all | bytes 655360 | tf_op jit(solution)/shard_map/to_masters/all_to_all | solution.py:232
  60.0 0.6 masters.1
  60.6 27.4 %all_to_all.16.got_ref = bf16[32,40,128]{2,1,0:T(8,128)(2,1)S(1)} all-to-all(bf16[32,40,128]{2,1,0:T(8,128)(2,1)S(1)} %get-tuple-element.14), channel_id=1, replica_groups={{272,0,16,32,48,64,80,96,112,128,144,160,176,192,208,224,240,256,288,30..., dimensions={0} | all-to-all | bytes 655360 | tf_op jit(solution)/shard_map/to_mirrors/all_to_all | solution.py:245
  87.9 1.7 %mirrors.1 = (bf16[32,4096]{1,0:T(8,128)(2,1)}, f32[32,512]{1,0:T(8,128)}, bf16[32,768]{1,0:T(8,128)(2,1)}) custom-call(s32[1,32]{1,0:T(1,128)} %owner_hbm.3, bf16[32,40,128]{2,1,0:T(8,128)(2,1)S(1)} %all_to_all.16.got_ref, bf16[32,768]{1,0:T(8,128)(2,1)S(1)} %get-tuple-element.15.kept_ref), custom_call_target="tpu_custom_call" | custom-call | tf_op jit(solution)/shard_map/mirrors/pallas_call | solution.py:246
Async XLA Ops:
  2.4 16.2 %all-to-all-start = ((bf16[16,32,768]{2,1,0:T(8,128)(2,1)}), bf16[16,32,768]{2,1,0:T(8,128)(2,1)}, u32[]{:S(2)}, u32[]{:S(2)}) async-start(bf16[16,32,768]{2,1,0:T(8,128)(2,1)} %spread.1), calls=%async_computation | async-start | bytes 1572864 | tf_op jit(solution)/shard_map/gather_features/all_to_all | solution.py:193

commit v5 on v4

v5 whole, which is shorter than its diff:
```python
import functools

import jax
import jax.numpy as jnp
from jax import lax
from jax.experimental import pallas as pl
from jax.experimental.pallas import tpu as pltpu
from jax.sharding import PartitionSpec as P

LANES = 128
GROUP = 16
EARLY = 80
EXTRA = 6
VMEM_BYTES = 16 * 1024 * 1024
DOM_FIRST = 17
FEAT_FIRST = 10


def order_of(first, count):
    return [first] + [k for k in range(count) if k != first]


def place_of(index, first):
    return jnp.where(index == first, 0, index + (index < first).astype(jnp.int32))


def spread_kernel(source_hbm, copies_ref, source_ref, sem):
    move = pltpu.make_async_copy(source_hbm, source_ref, sem.at[0])
    move.start()
    move.wait()
    value = source_ref[...]
    for k in range(copies_ref.shape[0]):
        copies_ref[k] = value


def prefetch_kernel(
    dst_hbm, slot_hbm, count_ref, owner_hbm, local_hbm, weight_hbm, agg_hbm, tiles_hbm,
    dst_ref, place_ref, peer_ref, number_ref, weight_ref, agg_ref, tiles_ref,
    slot_ref, owner_ref, local_ref, sems,
):
    pairs = (
        (owner_hbm, owner_ref), (local_hbm, local_ref), (slot_hbm, slot_ref), (dst_hbm, dst_ref),
        (weight_hbm, weight_ref), (agg_hbm, agg_ref), (tiles_hbm.at[pl.ds(0, EARLY)], tiles_ref),
    )
    moves = [pltpu.make_async_copy(a, b, sems.at[k]) for k, (a, b) in enumerate(pairs)]
    for move in moves:
        move.start()
    peers = peer_ref.shape[0]
    tile_total = place_ref.shape[0]
    moves[0].wait()
    moves[1].wait()

    def slot_step(s, carry):
        place = place_of(owner_ref[0, s], DOM_FIRST)
        peer_ref[s] = place
        number_ref[place] = local_ref[0, s]
        return carry

    lax.fori_loop(0, peers, slot_step, 0)
    moves[2].wait()
    count = count_ref[0]

    def tile_step(t, carry):
        place_ref[t] = jnp.where(t < count, peer_ref[slot_ref[t]], peers)
        return carry

    lax.fori_loop(0, tile_total, tile_step, 0)
    for move in moves[3:]:
        move.wait()


def partial_kernel(
    dst_ref, place_ref, number_ref, piece_ref, weight_ref, agg_ref, early_ref, tiles_hbm,
    msg_ref,
    back_ref, acc_ref, extra_ref, late_ref, sems,
):
    block_count, rows, _ = back_ref.shape
    peers = msg_ref.shape[0]
    msg_ref = msg_ref.reshape(peers, msg_ref.shape[1] * msg_ref.shape[2], LANES)
    tile_total = tiles_hbm.shape[0]
    wide = weight_ref.shape[1] // LANES
    late = pltpu.make_async_copy(
        tiles_hbm.at[pl.ds(EARLY, tile_total - EARLY)], late_ref, sems.at[0]
    )
    late.start()
    acc_ref[...] = jnp.zeros_like(acc_ref)
    groups = piece_ref.shape[0]
    piece = jnp.concatenate(
        [piece_ref[k] for k in range(1, FEAT_FIRST + 1)]
        + [piece_ref[0]]
        + [piece_ref[k] for k in range(FEAT_FIRST + 1, groups)],
        axis=0,
    )
    back = jnp.dot(weight_ref[...], piece, preferred_element_type=jnp.float32)
    back = back.astype(jnp.bfloat16)
    for b in range(block_count):
        back_ref[b] = back[:, b * LANES : (b + 1) * LANES]
    term = lax.dot_general(
        agg_ref[...], piece, (((1,), (1,)), ((), ())), preferred_element_type=jnp.float32
    )
    for k in range(wide):
        extra_ref[:, k, :] = term[:, k * LANES : (k + 1) * LANES]
    extra_ref[:, wide:, :] = jnp.zeros_like(extra_ref[:, wide:, :])
    for k in range(peers):
        value = number_ref[k].astype(jnp.float32)
        extra_ref[k, pl.ds(wide, 1), :] = jnp.full((1, LANES), value, jnp.float32)
    msg_ref[:, rows:, :] = extra_ref[:, :EXTRA, :].astype(jnp.bfloat16)
    for start in range(0, tile_total, GROUP):
        if start == EARLY:
            late.wait()
        products, places = [], []
        for t in range(start, min(start + GROUP, tile_total)):
            tile = early_ref[t] if t < EARLY else late_ref[t - EARLY]
            products.append(
                jnp.dot(back_ref[dst_ref[t]], tile, preferred_element_type=jnp.float32)
            )
            places.append(place_ref[t])
        for place, product in zip(places, products):
            acc_ref[place] += product
    msg_ref[:, :rows, :] = acc_ref[:peers].astype(jnp.bfloat16)


def master_kernel(wide, got_ref, nodes_ref, msg_ref):
    peers = got_ref.shape[0]
    got_ref = got_ref.reshape(peers, got_ref.shape[1] * got_ref.shape[2], LANES)
    rows, columns = nodes_ref.shape
    block_count = columns // LANES
    msg_ref = msg_ref.reshape(peers, rows + wide, LANES)
    tail = got_ref[:, rows:, :].astype(jnp.float32)
    numbers = [tail[p, wide : wide + 1, :] for p in range(peers)]
    sums = [jnp.zeros((rows, LANES), jnp.float32) for _ in range(block_count)]
    for p in range(peers):
        part = got_ref[p, :rows, :].astype(jnp.float32)
        for b in range(block_count):
            sums[b] = sums[b] + jnp.where(numbers[p] == float(b), part, 0.0)
    for b in range(block_count):
        nodes_ref[:, b * LANES : (b + 1) * LANES] = sums[b].astype(jnp.bfloat16)
    for p in range(peers):
        pick = sums[0]
        for b in range(1, block_count):
            pick = jnp.where(numbers[p] == float(b), sums[b], pick)
        msg_ref[p, :rows, :] = pick.astype(jnp.bfloat16)
    total = jnp.sum(tail, axis=0)[:wide].astype(jnp.bfloat16)
    for p in range(peers):
        msg_ref[p, rows:, :] = total


def mirror_kernel(
    wide, peer_ref, got_ref, kept_ref, mirrors_hbm, wgrad_hbm, nodes_hbm,
    wgrad_ref, mirrors_ref, sems,
):
    peers = got_ref.shape[0]
    rows = wgrad_ref.shape[0]
    got_ref = got_ref.reshape(peers, rows + wide, LANES)
    moves = [pltpu.make_async_copy(kept_ref, nodes_hbm, sems.at[1])]
    moves[0].start()
    tail = got_ref[:, rows:, :].astype(jnp.float32)
    for k in range(wide):
        wgrad_ref[:, k * LANES : (k + 1) * LANES] = tail[:, k, :]
    moves.append(pltpu.make_async_copy(wgrad_ref, wgrad_hbm, sems.at[2]))
    moves[1].start()
    part = peers // 2
    for c in range(2):
        for s in range(c * part, (c + 1) * part):
            mirrors_ref[:, s * LANES : (s + 1) * LANES] = got_ref[peer_ref[s], :rows, :]
        span = pl.ds(c * part * LANES, part * LANES)
        move = pltpu.make_async_copy(mirrors_ref.at[:, span], mirrors_hbm.at[:, span], sems.at[3 + c])
        move.start()
        moves.append(move)
    for move in moves:
        move.wait()


def in_hbm(array):
    return pltpu.with_memory_space_constraint(array, pltpu.HBM)


def in_vmem(array):
    return pltpu.with_memory_space_constraint(array, pltpu.VMEM)


def body(
    grad_out,
    saved_agg,
    weight,
    tile_values,
    tile_dst,
    tile_slot,
    tile_count,
    mirror_owner,
    mirror_local,
):
    rows, columns = grad_out.shape
    block_count = columns // LANES
    peers = mirror_owner.shape[1]
    features = weight.shape[1]
    wide = features // LANES
    groups = features // rows
    height = rows + EXTRA
    dom_groups = [order_of(DOM_FIRST, peers)]
    vmem = pl.BlockSpec(memory_space=pltpu.VMEM)
    smem = pl.BlockSpec(memory_space=pltpu.SMEM)
    hbm = pl.BlockSpec(memory_space=pltpu.HBM)
    params = pltpu.CompilerParams(vmem_limit_bytes=VMEM_BYTES)

    copies = pl.pallas_call(
        spread_kernel,
        out_shape=pltpu.VMEM((groups, rows, columns), grad_out.dtype),
        in_specs=[hbm],
        out_specs=vmem,
        scratch_shapes=[pltpu.VMEM(grad_out.shape, grad_out.dtype), pltpu.SemaphoreType.DMA((1,))],
        compiler_params=params,
        name="spread",
    )(in_hbm(grad_out))
    with jax.named_scope("gather_features"):
        piece = lax.all_to_all(
            copies, "feat", 0, 0, tiled=True, axis_index_groups=[order_of(FEAT_FIRST, groups)]
        )
    operands = (weight, saved_agg, tile_values)
    dst, place, peer, number, *near = pl.pallas_call(
        prefetch_kernel,
        out_shape=(
            pltpu.SMEM(tile_dst.shape, jnp.int32),
            pltpu.SMEM(tile_slot.shape, jnp.int32),
            pltpu.SMEM((peers,), jnp.int32),
            pltpu.SMEM((peers,), jnp.int32),
            *(pltpu.VMEM(x.shape, x.dtype) for x in operands[:2]),
            pltpu.VMEM((EARLY, LANES, LANES), tile_values.dtype),
        ),
        in_specs=[hbm] * 2 + [smem] + [hbm] * 5,
        out_specs=(smem,) * 4 + (vmem,) * 3,
        scratch_shapes=[
            pltpu.SMEM(tile_slot.shape, jnp.int32),
            pltpu.SMEM(mirror_owner.shape, jnp.int32),
            pltpu.SMEM(mirror_local.shape, jnp.int32),
            pltpu.SemaphoreType.DMA((7,)),
        ],
        compiler_params=params,
        cost_estimate=pl.CostEstimate(
            flops=0, transcendentals=0, bytes_accessed=2 * sum(x.size * 2 for x in operands)
        ),
        name="prefetch",
    )(
        in_hbm(tile_dst), in_hbm(tile_slot), tile_count, in_hbm(mirror_owner), in_hbm(mirror_local),
        *map(in_hbm, operands),
    )
    message = pl.pallas_call(
        partial_kernel,
        out_shape=pltpu.VMEM((peers, height // 2, 2, LANES), jnp.bfloat16),
        in_specs=[smem] * 3 + [vmem] * 4 + [hbm],
        out_specs=vmem,
        scratch_shapes=[
            pltpu.VMEM((block_count, rows, LANES), jnp.bfloat16),
            pltpu.VMEM((peers + 1, rows, LANES), jnp.float32),
            pltpu.VMEM((peers, 8, LANES), jnp.float32),
            pltpu.VMEM((tile_values.shape[0] - EARLY, LANES, LANES), tile_values.dtype),
            pltpu.SemaphoreType.DMA((1,)),
        ],
        compiler_params=params,
        name="partials",
    )(dst, place, number, piece, *map(in_vmem, near), in_hbm(tile_values))
    with jax.named_scope("to_masters"):
        got = lax.all_to_all(message, "dom", 0, 0, tiled=True, axis_index_groups=dom_groups)
    kept, answer = pl.pallas_call(
        functools.partial(master_kernel, wide),
        out_shape=(
            pltpu.VMEM((rows, columns), jnp.bfloat16),
            pltpu.VMEM((peers, (rows + wide) // wide, wide, LANES), jnp.bfloat16),
        ),
        in_specs=[vmem],
        out_specs=(vmem, vmem),
        compiler_params=params,
        name="masters",
    )(got)
    with jax.named_scope("to_mirrors"):
        back = lax.all_to_all(answer, "dom", 0, 0, tiled=True, axis_index_groups=dom_groups)
    grad_mirrors, weight_grad, grad_nodes = pl.pallas_call(
        functools.partial(mirror_kernel, wide),
        out_shape=(
            pltpu.HBM((rows, peers * LANES), jnp.bfloat16),
            pltpu.HBM((rows, features), jnp.float32),
            pltpu.HBM((rows, columns), jnp.bfloat16),
        ),
        in_specs=[smem, vmem, vmem],
        out_specs=(hbm, hbm, hbm),
        scratch_shapes=[
            pltpu.VMEM((rows, features), jnp.float32),
            pltpu.VMEM((rows, peers * LANES), jnp.bfloat16),
            pltpu.SemaphoreType.DMA((3 + 2,)),
        ],
        compiler_params=params,
        name="mirrors",
    )(peer, back, kept)
    return (grad_nodes, grad_mirrors, weight_grad)


def solution(mesh):
    in_specs = (
        P("feat", "dom"),
        P("feat", "dom"),
        P("feat", None),
        P("dom", None, None),
        P("dom"),
        P("dom"),
        P("dom"),
        P("dom", None),
        P("dom", None),
    )
    out_specs = (P("feat", "dom"), P("feat", "dom"), P("feat", None))
    return jax.shard_map(body, mesh=mesh, in_specs=in_specs, out_specs=out_specs, check_vma=False)
```

time: 90 us -> 86 us (0.956)
  blocking collectives: 65.5 us -> 63.6 us
  Pallas kernels: 9.26 us -> 7.83 us
    all_to_all x1, blocking collectives: 27.4 us -> 26 us  [body(): lax.all_to_all(answer, 'dom', 0, 0, tiled=True, axis_index_groups=dom_gro...]
where the time goes in v5:
time: 86 us; the launch traced here: 85.6 us
  blocking collectives  63.6 us (74%)
  starting transfers between devices  9.62 us (11%)
  Pallas kernels  7.83 us (9%)
  waiting for transfers between devices  3.22 us (4%)
  between operations  1.31 us (2%)
    all_to_all x1, blocking collectives, body(): lax.all_to_all(message, 'dom', 0, 0, tiled=True, axis_index_groups=dom_gr...  37.6 us
    all_to_all x1, blocking collectives, body(): lax.all_to_all(answer, 'dom', 0, 0, tiled=True, axis_index_groups=dom_gro...  26 us
    all_to_all x1, starting transfers between devices, body(): lax.all_to_all(copies, 'feat', 0, 0, tiled=True, axis_index_groups=[order...  9.62 us
    all_to_all x1, waiting for transfers between devices, body(): lax.all_to_all(copies, 'feat', 0, 0, tiled=True, axis_index_groups=[order...  3.22 us
    pallas_call x1, Pallas kernels, body(): pl.pallas_call(partial_kernel, out_shape=pltpu.VMEM((peers, height // 2,...  2.59 us
    pallas_call x1, Pallas kernels, body(): pl.pallas_call(prefetch_kernel, out_shape=(pltpu.SMEM(tile_dst.shape, jnp...  1.86 us
    pallas_call x1, Pallas kernels, body(): pl.pallas_call(spread_kernel, out_shape=pltpu.VMEM((groups, rows, columns...  1.77 us
  transfers between devices with their start and end apart: 1, of which 1 were waited for; matrix products, arithmetic and copies ran while one was open for 0% of the time, Pallas kernels for 2%

profile of v5, /device:TPU:1, one launch (start us, length us, event | category | flops | bytes accessed | tf_op | source)
XLA Modules:
  0.0 85.6 jit_solution(18258736140250815223)
XLA Ops:
  0.6 1.8 %spread.1 = bf16[16,32,768]{2,1,0:T(8,128)(2,1)} custom-call(bf16[32,768]{1,0:T(8,128)(2,1)} %source_hbm.1), custom_call_target="tpu_custom_call" | custom-call | tf_op jit(solution)/shard_map/spread/pallas_call | solution.py:206
  2.4 9.6 %all-to-all-start = ((bf16[16,32,768]{2,1,0:T(8,128)(2,1)}), bf16[16,32,768]{2,1,0:T(8,128)(2,1)S(1)}, u32[]{:S(2)}, u32[]{:S(2)}) async-start(bf16[16,32,768]{2,1,0:T(8,128)(2,1)} %spread.1), calls=%async_computation | async-start | bytes 1572864 | tf_op jit(solution)/shard_map/gather_features/all_to_all | solution.py:216
  12.7 1.9 %prefetch.1 = (s32[96]{0:T(128)S(4)}, s32[96]{0:T(128)S(4)}, s32[32]{0:T(128)S(4)}, s32[32]{0:T(128)S(4)}, bf16[32,512]{1,0:T(8,128)(2,1)S(1)}, /*index=5*/bf16[...) custom-call(s32[96]{0:T(128)} %dst_hbm.1, s32[96]{0:T(128)} %slot_hbm.1, s32[1]{0:T(128)S(6)} %copy.12.count_ref, ...), custom_call_target="tpu_custom_call" | custom-call | bytes 6455296 | tf_op jit(solution)/shard_map/prefetch/pallas_call | solution.py:220
  14.5 3.2 %all-to-all-done.piece_ref = bf16[16,32,768]{2,1,0:T(8,128)(2,1)S(1)} async-done(((bf16[16,32,768]{2,1,0:T(8,128)(2,1)}), bf16[16,32,768]{2,1,0:T(8,128)(2,1)S(1)}, u32[]{:S(2)}, u32[]{:S(2)}) %all-to-all-start) | async-done | bytes 786464 | tf_op jit(solution)/shard_map/gather_features/all_to_all | solution.py:216
  17.8 2.6 %partials.1 = bf16[32,19,2,128]{3,2,1,0:T(2,128)(2,1)S(1)} custom-call(s32[96]{0:T(128)S(4)} %get-tuple-element.16.dst_ref, s32[96]{0:T(128)S(4)} %get-tuple-element.17.place_ref, s32[32]{0:T(128)S(4)} %get-tuple-element.18.number_ref, bf16[16,32,768]{2,1,0:T(8,128)(2,1)S(1)} %all-to-all-done.piece_ref, bf16[32,512]{1,0:T(8,128)(2,1)S(1)} %get-tuple-element.19.weight_ref, ...), custom_call_target="tpu_custom_call" | custom-call | tf_op jit(solution)/shard_map/partials/pallas_call | solution.py:247
  20.4 37.6 %all_to_all.15.got_ref = bf16[32,19,2,128]{3,2,1,0:T(2,128)(2,1)S(1)} all-to-all(bf16[32,19,2,128]{3,2,1,0:T(2,128)(2,1)S(1)} %partials.1), channel_id=1, replica_groups={{272,0,16,32,48,64,80,96,112,128,144,160,176,192,208,224,240,256,288,30..., dimensions={0} | all-to-all | bytes 622592 | tf_op jit(solution)/shard_map/to_masters/all_to_all | solution.py:263
  57.9 0.8 masters.1
  58.7 26.0 %all_to_all.16.got_ref = bf16[32,9,4,128]{3,2,1,0:T(4,128)(2,1)S(1)} all-to-all(bf16[32,9,4,128]{3,2,1,0:T(4,128)(2,1)S(1)} %get-tuple-element.22), channel_id=1, replica_groups={{272,0,16,32,48,64,80,96,112,128,144,160,176,192,208,224,240,256,288,30..., dimensions={0} | all-to-all | bytes 589824 | tf_op jit(solution)/shard_map/to_mirrors/all_to_all | solution.py:276
  84.7 0.8 mirrors.1
Async XLA Ops:
  2.4 15.4 %all-to-all-start = ((bf16[16,32,768]{2,1,0:T(8,128)(2,1)}), bf16[16,32,768]{2,1,0:T(8,128)(2,1)S(1)}, u32[]{:S(2)}, u32[]{:S(2)}) async-start(bf16[16,32,768]{2,1,0:T(8,128)(2,1)} %spread.1), calls=%async_computation | async-start | bytes 1572864 | tf_op jit(solution)/shard_map/gather_features/all_to_all | solution.py:216

commit v6 on v5

--- a/solution.py
+++ b/solution.py
@@ -8,7 +8,7 @@
 from jax.sharding import PartitionSpec as P
 
 LANES = 128
-GROUP = 16
+GROUP = 40
 EARLY = 80
 EXTRA = 6
 VMEM_BYTES = 16 * 1024 * 1024
@@ -105,18 +105,26 @@
         value = number_ref[k].astype(jnp.float32)
         extra_ref[k, pl.ds(wide, 1), :] = jnp.full((1, LANES), value, jnp.float32)
     msg_ref[:, rows:, :] = extra_ref[:, :EXTRA, :].astype(jnp.bfloat16)
-    for start in range(0, tile_total, GROUP):
-        if start == EARLY:
-            late.wait()
+    def add_tiles(start, count, tiles_ref, skip):
         products, places = [], []
-        for t in range(start, min(start + GROUP, tile_total)):
-            tile = early_ref[t] if t < EARLY else late_ref[t - EARLY]
+        for t in range(count):
             products.append(
-                jnp.dot(back_ref[dst_ref[t]], tile, preferred_element_type=jnp.float32)
+                jnp.dot(
+                    back_ref[dst_ref[start + t]], tiles_ref[start + t - skip],
+                    preferred_element_type=jnp.float32,
+                )
             )
-            places.append(place_ref[t])
+            places.append(place_ref[start + t])
         for place, product in zip(places, products):
             acc_ref[place] += product
+
+    def step(i, carry):
+        add_tiles(i * GROUP, GROUP, early_ref, 0)
+        return carry
+
+    lax.fori_loop(0, EARLY // GROUP, step, 0)
+    late.wait()
+    add_tiles(EARLY, tile_total - EARLY, late_ref, EARLY)
     msg_ref[:, :rows, :] = acc_ref[:peers].astype(jnp.bfloat16)
 
 

time: 86 us -> 85.2 us (level)
  no operation moved by 1% of the time
where the time goes in v6:
time: 85.2 us; the launch traced here: 84.9 us
  blocking collectives  63.6 us (75%)
  starting transfers between devices  9.62 us (11%)
  Pallas kernels  7.15 us (8%)
  waiting for transfers between devices  3.22 us (4%)
  between operations  1.31 us (2%)
    all_to_all x1, blocking collectives, body(): lax.all_to_all(message, 'dom', 0, 0, tiled=True, axis_index_groups=dom_gr...  37.6 us
    all_to_all x1, blocking collectives, body(): lax.all_to_all(answer, 'dom', 0, 0, tiled=True, axis_index_groups=dom_gro...  26 us
    all_to_all x1, starting transfers between devices, body(): lax.all_to_all(copies, 'feat', 0, 0, tiled=True, axis_index_groups=[order...  9.62 us
    all_to_all x1, waiting for transfers between devices, body(): lax.all_to_all(copies, 'feat', 0, 0, tiled=True, axis_index_groups=[order...  3.22 us
    pallas_call x1, Pallas kernels, body(): pl.pallas_call(partial_kernel, out_shape=pltpu.VMEM((peers, height // 2,...  1.92 us
    pallas_call x1, Pallas kernels, body(): pl.pallas_call(prefetch_kernel, out_shape=(pltpu.SMEM(tile_dst.shape, jnp...  1.86 us
    pallas_call x1, Pallas kernels, body(): pl.pallas_call(spread_kernel, out_shape=pltpu.VMEM((groups, rows, columns...  1.77 us
  transfers between devices with their start and end apart: 1, of which 1 were waited for; matrix products, arithmetic and copies ran while one was open for 0% of the time, Pallas kernels for 2%

profile of v6, /device:TPU:1, one launch (start us, length us, event | category | flops | bytes accessed | tf_op | source)
XLA Modules:
  0.0 84.9 jit_solution(11191262736673003991)
XLA Ops:
  0.6 1.8 %spread.1 = bf16[16,32,768]{2,1,0:T(8,128)(2,1)} custom-call(bf16[32,768]{1,0:T(8,128)(2,1)} %source_hbm.1), custom_call_target="tpu_custom_call" | custom-call | tf_op jit(solution)/shard_map/spread/pallas_call | solution.py:214
  2.4 9.6 %all-to-all-start = ((bf16[16,32,768]{2,1,0:T(8,128)(2,1)}), bf16[16,32,768]{2,1,0:T(8,128)(2,1)S(1)}, u32[]{:S(2)}, u32[]{:S(2)}) async-start(bf16[16,32,768]{2,1,0:T(8,128)(2,1)} %spread.1), calls=%async_computation | async-start | bytes 1572864 | tf_op jit(solution)/shard_map/gather_features/all_to_all | solution.py:224
  12.7 1.9 %prefetch.1 = (s32[96]{0:T(128)S(4)}, s32[96]{0:T(128)S(4)}, s32[32]{0:T(128)S(4)}, s32[32]{0:T(128)S(4)}, bf16[32,512]{1,0:T(8,128)(2,1)S(1)}, /*index=5*/bf16[...) custom-call(s32[96]{0:T(128)} %dst_hbm.1, s32[96]{0:T(128)} %slot_hbm.1, s32[1]{0:T(128)S(6)} %copy.12.count_ref, ...), custom_call_target="tpu_custom_call" | custom-call | bytes 6455296 | tf_op jit(solution)/shard_map/prefetch/pallas_call | solution.py:228
  14.5 3.2 %all-to-all-done.piece_ref = bf16[16,32,768]{2,1,0:T(8,128)(2,1)S(1)} async-done(((bf16[16,32,768]{2,1,0:T(8,128)(2,1)}), bf16[16,32,768]{2,1,0:T(8,128)(2,1)S(1)}, u32[]{:S(2)}, u32[]{:S(2)}) %all-to-all-start) | async-done | bytes 786464 | tf_op jit(solution)/shard_map/gather_features/all_to_all | solution.py:224
  17.8 1.9 %partials.1 = bf16[32,19,2,128]{3,2,1,0:T(2,128)(2,1)S(1)} custom-call(s32[96]{0:T(128)S(4)} %get-tuple-element.16.dst_ref, s32[96]{0:T(128)S(4)} %get-tuple-element.17.place_ref, s32[32]{0:T(128)S(4)} %get-tuple-element.18.number_ref, bf16[16,32,768]{2,1,0:T(8,128)(2,1)S(1)} %all-to-all-done.piece_ref, bf16[32,512]{1,0:T(8,128)(2,1)S(1)} %get-tuple-element.19.weight_ref, ...), custom_call_target="tpu_custom_call" | custom-call | tf_op jit(solution)/shard_map/partials/pallas_call | solution.py:255
  19.7 37.6 %all_to_all.15.got_ref = bf16[32,19,2,128]{3,2,1,0:T(2,128)(2,1)S(1)} all-to-all(bf16[32,19,2,128]{3,2,1,0:T(2,128)(2,1)S(1)} %partials.1), channel_id=1, replica_groups={{272,0,16,32,48,64,80,96,112,128,144,160,176,192,208,224,240,256,288,30..., dimensions={0} | all-to-all | bytes 622592 | tf_op jit(solution)/shard_map/to_masters/all_to_all | solution.py:271
  57.3 0.8 masters.1
  58.0 26.0 %all_to_all.16.got_ref = bf16[32,9,4,128]{3,2,1,0:T(4,128)(2,1)S(1)} all-to-all(bf16[32,9,4,128]{3,2,1,0:T(4,128)(2,1)S(1)} %get-tuple-element.22), channel_id=1, replica_groups={{272,0,16,32,48,64,80,96,112,128,144,160,176,192,208,224,240,256,288,30..., dimensions={0} | all-to-all | bytes 589824 | tf_op jit(solution)/shard_map/to_mirrors/all_to_all | solution.py:284
  84.0 0.8 mirrors.1
Async XLA Ops:
  2.4 15.4 %all-to-all-start = ((bf16[16,32,768]{2,1,0:T(8,128)(2,1)}), bf16[16,32,768]{2,1,0:T(8,128)(2,1)S(1)}, u32[]{:S(2)}, u32[]{:S(2)}) async-start(bf16[16,32,768]{2,1,0:T(8,128)(2,1)} %spread.1), calls=%async_computation | async-start | bytes 1572864 | tf_op jit(solution)/shard_map/gather_features/all_to_all | solution.py:224

commit v7 on v5

--- a/solution.py
+++ b/solution.py
@@ -8,8 +8,7 @@
 from jax.sharding import PartitionSpec as P
 
 LANES = 128
-GROUP = 16
-EARLY = 80
+GROUP = 48
 EXTRA = 6
 VMEM_BYTES = 16 * 1024 * 1024
 DOM_FIRST = 17
@@ -24,23 +23,15 @@
     return jnp.where(index == first, 0, index + (index < first).astype(jnp.int32))
 
 
-def spread_kernel(source_hbm, copies_ref, source_ref, sem):
-    move = pltpu.make_async_copy(source_hbm, source_ref, sem.at[0])
-    move.start()
-    move.wait()
-    value = source_ref[...]
-    for k in range(copies_ref.shape[0]):
-        copies_ref[k] = value
-
-
-def prefetch_kernel(
-    dst_hbm, slot_hbm, count_ref, owner_hbm, local_hbm, weight_hbm, agg_hbm, tiles_hbm,
-    dst_ref, place_ref, peer_ref, number_ref, weight_ref, agg_ref, tiles_ref,
-    slot_ref, owner_ref, local_ref, sems,
+def stage_kernel(
+    grad_hbm, dst_hbm, slot_hbm, count_ref, owner_hbm, local_hbm, weight_hbm, agg_hbm, tiles_hbm,
+    copies_ref, dst_ref, place_ref, peer_ref, number_ref, weight_ref, agg_ref, tiles_ref,
+    grad_ref, slot_ref, owner_ref, local_ref, sems,
 ):
     pairs = (
-        (owner_hbm, owner_ref), (local_hbm, local_ref), (slot_hbm, slot_ref), (dst_hbm, dst_ref),
-        (weight_hbm, weight_ref), (agg_hbm, agg_ref), (tiles_hbm.at[pl.ds(0, EARLY)], tiles_ref),
+        (grad_hbm, grad_ref), (owner_hbm, owner_ref), (local_hbm, local_ref),
+        (slot_hbm, slot_ref), (dst_hbm, dst_ref),
+        (weight_hbm, weight_ref), (agg_hbm, agg_ref), (tiles_hbm, tiles_ref),
     )
     moves = [pltpu.make_async_copy(a, b, sems.at[k]) for k, (a, b) in enumerate(pairs)]
     for move in moves:
@@ -48,7 +39,11 @@
     peers = peer_ref.shape[0]
     tile_total = place_ref.shape[0]
     moves[0].wait()
+    value = grad_ref[...]
+    for k in range(copies_ref.shape[0]):
+        copies_ref[k] = value
     moves[1].wait()
+    moves[2].wait()
 
     def slot_step(s, carry):
         place = place_of(owner_ref[0, s], DOM_FIRST)
@@ -56,33 +51,29 @@
         number_ref[place] = local_ref[0, s]
         return carry
 
-    lax.fori_loop(0, peers, slot_step, 0)
-    moves[2].wait()
+    lax.fori_loop(0, peers, slot_step, 0, unroll=8)
+    moves[3].wait()
     count = count_ref[0]
 
     def tile_step(t, carry):
         place_ref[t] = jnp.where(t < count, peer_ref[slot_ref[t]], peers)
         return carry
 
-    lax.fori_loop(0, tile_total, tile_step, 0)
-    for move in moves[3:]:
+    lax.fori_loop(0, tile_total, tile_step, 0, unroll=8)
+    for move in moves[4:]:
         move.wait()
 
 
 def partial_kernel(
-    dst_ref, place_ref, number_ref, piece_ref, weight_ref, agg_ref, early_ref, tiles_hbm,
+    dst_ref, place_ref, number_ref, piece_ref, weight_ref, agg_ref, tiles_ref,
     msg_ref,
-    back_ref, acc_ref, extra_ref, late_ref, sems,
+    back_ref, acc_ref, extra_ref,
 ):
     block_count, rows, _ = back_ref.shape
     peers = msg_ref.shape[0]
     msg_ref = msg_ref.reshape(peers, msg_ref.shape[1] * msg_ref.shape[2], LANES)
-    tile_total = tiles_hbm.shape[0]
+    tile_total = tiles_ref.shape[0]
     wide = weight_ref.shape[1] // LANES
-    late = pltpu.make_async_copy(
-        tiles_hbm.at[pl.ds(EARLY, tile_total - EARLY)], late_ref, sems.at[0]
-    )
-    late.start()
     acc_ref[...] = jnp.zeros_like(acc_ref)
     groups = piece_ref.shape[0]
     piece = jnp.concatenate(
@@ -106,13 +97,10 @@
         extra_ref[k, pl.ds(wide, 1), :] = jnp.full((1, LANES), value, jnp.float32)
     msg_ref[:, rows:, :] = extra_ref[:, :EXTRA, :].astype(jnp.bfloat16)
     for start in range(0, tile_total, GROUP):
-        if start == EARLY:
-            late.wait()
         products, places = [], []
         for t in range(start, min(start + GROUP, tile_total)):
-            tile = early_ref[t] if t < EARLY else late_ref[t - EARLY]
             products.append(
-                jnp.dot(back_ref[dst_ref[t]], tile, preferred_element_type=jnp.float32)
+                jnp.dot(back_ref[dst_ref[t]], tiles_ref[t], preferred_element_type=jnp.float32)
             )
             places.append(place_ref[t])
         for place, product in zip(places, products):
@@ -175,10 +163,6 @@
     return pltpu.with_memory_space_constraint(array, pltpu.HBM)
 
 
-def in_vmem(array):
-    return pltpu.with_memory_space_constraint(array, pltpu.VMEM)
-
-
 def body(
     grad_out,
     saved_agg,
@@ -203,62 +187,49 @@
     hbm = pl.BlockSpec(memory_space=pltpu.HBM)
     params = pltpu.CompilerParams(vmem_limit_bytes=VMEM_BYTES)
 
-    copies = pl.pallas_call(
-        spread_kernel,
-        out_shape=pltpu.VMEM((groups, rows, columns), grad_out.dtype),
-        in_specs=[hbm],
-        out_specs=vmem,
-        scratch_shapes=[pltpu.VMEM(grad_out.shape, grad_out.dtype), pltpu.SemaphoreType.DMA((1,))],
-        compiler_params=params,
-        name="spread",
-    )(in_hbm(grad_out))
+    operands = (weight, saved_agg, tile_values)
+    copies, dst, place, peer, number, *near = pl.pallas_call(
+        stage_kernel,
+        out_shape=(
+            pltpu.VMEM((groups, rows, columns), grad_out.dtype),
+            pltpu.SMEM(tile_dst.shape, jnp.int32),
+            pltpu.SMEM(tile_slot.shape, jnp.int32),
+            pltpu.SMEM((peers,), jnp.int32),
+            pltpu.SMEM((peers,), jnp.int32),
+            *(pltpu.VMEM(x.shape, x.dtype) for x in operands),
+        ),
+        in_specs=[hbm] * 3 + [smem] + [hbm] * 5,
+        out_specs=(vmem,) + (smem,) * 4 + (vmem,) * 3,
+        scratch_shapes=[
+            pltpu.VMEM(grad_out.shape, grad_out.dtype),
+            pltpu.SMEM(tile_slot.shape, jnp.int32),
+            pltpu.SMEM(mirror_owner.shape, jnp.int32),
+            pltpu.SMEM(mirror_local.shape, jnp.int32),
+            pltpu.SemaphoreType.DMA((8,)),
+        ],
+        compiler_params=params,
+        name="stage",
+    )(
+        *map(in_hbm, (grad_out, tile_dst, tile_slot)), tile_count,
+        *map(in_hbm, (mirror_owner, mirror_local, *operands)),
+    )
     with jax.named_scope("gather_features"):
         piece = lax.all_to_all(
             copies, "feat", 0, 0, tiled=True, axis_index_groups=[order_of(FEAT_FIRST, groups)]
         )
-    operands = (weight, saved_agg, tile_values)
-    dst, place, peer, number, *near = pl.pallas_call(
-        prefetch_kernel,
-        out_shape=(
-            pltpu.SMEM(tile_dst.shape, jnp.int32),
-            pltpu.SMEM(tile_slot.shape, jnp.int32),
-            pltpu.SMEM((peers,), jnp.int32),
-            pltpu.SMEM((peers,), jnp.int32),
-            *(pltpu.VMEM(x.shape, x.dtype) for x in operands[:2]),
-            pltpu.VMEM((EARLY, LANES, LANES), tile_values.dtype),
-        ),
-        in_specs=[hbm] * 2 + [smem] + [hbm] * 5,
-        out_specs=(smem,) * 4 + (vmem,) * 3,
-        scratch_shapes=[
-            pltpu.SMEM(tile_slot.shape, jnp.int32),
-            pltpu.SMEM(mirror_owner.shape, jnp.int32),
-            pltpu.SMEM(mirror_local.shape, jnp.int32),
-            pltpu.SemaphoreType.DMA((7,)),
-        ],
-        compiler_params=params,
-        cost_estimate=pl.CostEstimate(
-            flops=0, transcendentals=0, bytes_accessed=2 * sum(x.size * 2 for x in operands)
-        ),
-        name="prefetch",
-    )(
-        in_hbm(tile_dst), in_hbm(tile_slot), tile_count, in_hbm(mirror_owner), in_hbm(mirror_local),
-        *map(in_hbm, operands),
-    )
     message = pl.pallas_call(
         partial_kernel,
         out_shape=pltpu.VMEM((peers, height // 2, 2, LANES), jnp.bfloat16),
-        in_specs=[smem] * 3 + [vmem] * 4 + [hbm],
+        in_specs=[smem] * 3 + [vmem] * 4,
         out_specs=vmem,
         scratch_shapes=[
             pltpu.VMEM((block_count, rows, LANES), jnp.bfloat16),
             pltpu.VMEM((peers + 1, rows, LANES), jnp.float32),
             pltpu.VMEM((peers, 8, LANES), jnp.float32),
-            pltpu.VMEM((tile_values.shape[0] - EARLY, LANES, LANES), tile_values.dtype),
-            pltpu.SemaphoreType.DMA((1,)),
         ],
         compiler_params=params,
         name="partials",
-    )(dst, place, number, piece, *map(in_vmem, near), in_hbm(tile_values))
+    )(dst, place, number, piece, *near)
     with jax.named_scope("to_masters"):
         got = lax.all_to_all(message, "dom", 0, 0, tiled=True, axis_index_groups=dom_groups)
     kept, answer = pl.pallas_call(

time: 86 us -> 84.9 us (0.987)
  blocking collectives: 63.6 us -> 78.2 us
  starting transfers between devices: 9.62 us -> 0 us
  waiting for transfers between devices: 3.22 us -> 0 us
  Pallas kernels: 7.83 us -> 5.16 us
    all_to_all x0 -> x1, blocking collectives: none -> 14.6 us  [body(): lax.all_to_all(copies, 'feat', 0, 0, tiled=True, axis_index_groups=[order...]
    all_to_all x1 -> x0, starting transfers between devices: 9.62 us -> none  [body(): lax.all_to_all(copies, 'feat', 0, 0, tiled=True, axis_index_groups=[order...]
    all_to_all x1 -> x0, waiting for transfers between devices: 3.22 us -> none  [body(): lax.all_to_all(copies, 'feat', 0, 0, tiled=True, axis_index_groups=[order...]
    pallas_call x2 -> x1, Pallas kernels: 3.63 us -> 2.04 us  [body(): pl.pallas_call(stage_kernel, out_shape=(pltpu.VMEM((groups, rows, columns...]
    pallas_call x1, Pallas kernels: 2.59 us -> 1.51 us  [body(): pl.pallas_call(partial_kernel, out_shape=pltpu.VMEM((peers, height // 2,...]
  transfers between devices with their start and end apart: 1 -> 0, of which waited for: 1 -> 0; matrix products, arithmetic and copies ran while one was open for 0% -> 0% of each run, Pallas kernels for 2% -> 0%
where the time goes in v7:
time: 84.9 us; the launch traced here: 84.6 us
  blocking collectives  78.2 us (92%)
  Pallas kernels  5.16 us (6%)
  between operations  1.3 us (2%)
    all_to_all x1, blocking collectives, body(): lax.all_to_all(message, 'dom', 0, 0, tiled=True, axis_index_groups=dom_gr...  37.6 us
    all_to_all x1, blocking collectives, body(): lax.all_to_all(answer, 'dom', 0, 0, tiled=True, axis_index_groups=dom_gro...  26 us
    all_to_all x1, blocking collectives, body(): lax.all_to_all(copies, 'feat', 0, 0, tiled=True, axis_index_groups=[order...  14.6 us
    pallas_call x1, Pallas kernels, body(): pl.pallas_call(stage_kernel, out_shape=(pltpu.VMEM((groups, rows, columns...  2.04 us

profile of v7, /device:TPU:1, one launch (start us, length us, event | category | flops | bytes accessed | tf_op | source)
XLA Modules:
  0.0 84.6 jit_solution(13510364833301147064)
XLA Ops:
  1.3 2.0 %stage.1 = (bf16[16,32,768]{2,1,0:T(8,128)(2,1)S(1)}, s32[96]{0:T(128)S(4)}, s32[96]{0:T(128)S(4)}, s32[32]{0:T(128)S(4)}, s32[32]{0:T(128)S(4)}, /*index=5*/bf1...) custom-call(bf16[32,768]{1,0:T(8,128)(2,1)} %grad_hbm.1, s32[96]{0:T(128)} %dst_hbm.1, ...), custom_call_target="tpu_custom_call" | custom-call | tf_op jit(solution)/shard_map/stage/pallas_call | solution.py:191
  3.3 14.6 %all_to_all.15.piece_ref = bf16[16,32,768]{2,1,0:T(8,128)(2,1)S(1)} all-to-all(bf16[16,32,768]{2,1,0:T(8,128)(2,1)S(1)} %get-tuple-element.20), channel_id=1, replica_groups={{10,0,1,2,3,4,5,6,7,8,9,11,12,13,14,15},{26,16,17,18,19,20,21,22,23,24,..., dimensions={0} | all-to-all | bytes 1572864 | tf_op jit(solution)/shard_map/gather_features/all_to_all | solution.py:217
  17.9 1.5 %partials.1 = bf16[32,19,2,128]{3,2,1,0:T(2,128)(2,1)S(1)} custom-call(s32[96]{0:T(128)S(4)} %get-tuple-element.17.dst_ref, s32[96]{0:T(128)S(4)} %get-tuple-element.18.place_ref, s32[32]{0:T(128)S(4)} %get-tuple-element.19.number_ref, bf16[16,32,768]{2,1,0:T(8,128)(2,1)S(1)} %all_to_all.15.piece_ref, bf16[32,512]{1,0:T(8,128)(2,1)S(1)} %get-tuple-element.21.weight_ref, ...), custom_call_target="tpu_custom_call" | custom-call | tf_op jit(solution)/shard_map/partials/pallas_call | solution.py:220
  19.4 37.6 %all_to_all.16.got_ref = bf16[32,19,2,128]{3,2,1,0:T(2,128)(2,1)S(1)} all-to-all(bf16[32,19,2,128]{3,2,1,0:T(2,128)(2,1)S(1)} %partials.1), channel_id=1, replica_groups={{272,0,16,32,48,64,80,96,112,128,144,160,176,192,208,224,240,256,288,30..., dimensions={0} | all-to-all | bytes 622592 | tf_op jit(solution)/shard_map/to_masters/all_to_all | solution.py:234
  57.0 0.8 masters.1
  57.8 26.0 %all_to_all.17.got_ref = bf16[32,9,4,128]{3,2,1,0:T(4,128)(2,1)S(1)} all-to-all(bf16[32,9,4,128]{3,2,1,0:T(4,128)(2,1)S(1)} %get-tuple-element.24), channel_id=1, replica_groups={{272,0,16,32,48,64,80,96,112,128,144,160,176,192,208,224,240,256,288,30..., dimensions={0} | all-to-all | bytes 589824 | tf_op jit(solution)/shard_map/to_mirrors/all_to_all | solution.py:247
  83.8 0.8 mirrors.1

commit v8 on v7

--- a/solution.py
+++ b/solution.py
@@ -11,7 +11,7 @@
 GROUP = 48
 EXTRA = 6
 VMEM_BYTES = 16 * 1024 * 1024
-DOM_FIRST = 17
+DOM_FIRST = 19
 FEAT_FIRST = 10
 
 
@@ -115,7 +115,7 @@
     block_count = columns // LANES
     msg_ref = msg_ref.reshape(peers, rows + wide, LANES)
     tail = got_ref[:, rows:, :].astype(jnp.float32)
-    numbers = [tail[p, wide : wide + 1, :] for p in range(peers)]
+    numbers = [jnp.broadcast_to(tail[p, wide : wide + 1, :], (rows, LANES)) for p in range(peers)]
     sums = [jnp.zeros((rows, LANES), jnp.float32) for _ in range(block_count)]
     for p in range(peers):
         part = got_ref[p, :rows, :].astype(jnp.float32)

time: 84.9 us -> 84.6 us (level)
  no operation moved by 1% of the time
where the time goes in v8:
time: 84.6 us; the launch traced here: 84.3 us
  blocking collectives  77.9 us (92%)
  Pallas kernels  5.1 us (6%)
  between operations  1.3 us (2%)
    all_to_all x1, blocking collectives, body(): lax.all_to_all(message, 'dom', 0, 0, tiled=True, axis_index_groups=dom_gr...  37.4 us
    all_to_all x1, blocking collectives, body(): lax.all_to_all(answer, 'dom', 0, 0, tiled=True, axis_index_groups=dom_gro...  26 us
    all_to_all x1, blocking collectives, body(): lax.all_to_all(copies, 'feat', 0, 0, tiled=True, axis_index_groups=[order...  14.6 us
    pallas_call x1, Pallas kernels, body(): pl.pallas_call(stage_kernel, out_shape=(pltpu.VMEM((groups, rows, columns...  2.04 us

profile of v8, /device:TPU:1, one launch (start us, length us, event | category | flops | bytes accessed | tf_op | source)
XLA Modules:
  0.0 84.3 jit_solution(10858216681414226402)
XLA Ops:
  1.3 2.0 %stage.1 = (bf16[16,32,768]{2,1,0:T(8,128)(2,1)S(1)}, s32[96]{0:T(128)S(4)}, s32[96]{0:T(128)S(4)}, s32[32]{0:T(128)S(4)}, s32[32]{0:T(128)S(4)}, /*index=5*/bf1...) custom-call(bf16[32,768]{1,0:T(8,128)(2,1)} %grad_hbm.1, s32[96]{0:T(128)} %dst_hbm.1, ...), custom_call_target="tpu_custom_call" | custom-call | tf_op jit(solution)/shard_map/stage/pallas_call | solution.py:191
  3.3 14.6 %all_to_all.15.piece_ref = bf16[16,32,768]{2,1,0:T(8,128)(2,1)S(1)} all-to-all(bf16[16,32,768]{2,1,0:T(8,128)(2,1)S(1)} %get-tuple-element.20), channel_id=1, replica_groups={{10,0,1,2,3,4,5,6,7,8,9,11,12,13,14,15},{26,16,17,18,19,20,21,22,23,24,..., dimensions={0} | all-to-all | bytes 1572864 | tf_op jit(solution)/shard_map/gather_features/all_to_all | solution.py:217
  17.9 1.5 %partials.1 = bf16[32,19,2,128]{3,2,1,0:T(2,128)(2,1)S(1)} custom-call(s32[96]{0:T(128)S(4)} %get-tuple-element.17.dst_ref, s32[96]{0:T(128)S(4)} %get-tuple-element.18.place_ref, s32[32]{0:T(128)S(4)} %get-tuple-element.19.number_ref, bf16[16,32,768]{2,1,0:T(8,128)(2,1)S(1)} %all_to_all.15.piece_ref, bf16[32,512]{1,0:T(8,128)(2,1)S(1)} %get-tuple-element.21.weight_ref, ...), custom_call_target="tpu_custom_call" | custom-call | tf_op jit(solution)/shard_map/partials/pallas_call | solution.py:220
  19.4 37.4 %all_to_all.16.got_ref = bf16[32,19,2,128]{3,2,1,0:T(2,128)(2,1)S(1)} all-to-all(bf16[32,19,2,128]{3,2,1,0:T(2,128)(2,1)S(1)} %partials.1), channel_id=1, replica_groups={{304,0,16,32,48,64,80,96,112,128,144,160,176,192,208,224,240,256,272,28..., dimensions={0} | all-to-all | bytes 622592 | tf_op jit(solution)/shard_map/to_masters/all_to_all | solution.py:234
  56.8 0.7 masters.1
  57.5 26.0 %all_to_all.17.got_ref = bf16[32,9,4,128]{3,2,1,0:T(4,128)(2,1)S(1)} all-to-all(bf16[32,9,4,128]{3,2,1,0:T(4,128)(2,1)S(1)} %get-tuple-element.24), channel_id=1, replica_groups={{304,0,16,32,48,64,80,96,112,128,144,160,176,192,208,224,240,256,272,28..., dimensions={0} | all-to-all | bytes 589824 | tf_op jit(solution)/shard_map/to_mirrors/all_to_all | solution.py:247
  83.5 0.8 mirrors.1

commit v9 on v8

--- a/solution.py
+++ b/solution.py
@@ -142,11 +142,6 @@
     got_ref = got_ref.reshape(peers, rows + wide, LANES)
     moves = [pltpu.make_async_copy(kept_ref, nodes_hbm, sems.at[1])]
     moves[0].start()
-    tail = got_ref[:, rows:, :].astype(jnp.float32)
-    for k in range(wide):
-        wgrad_ref[:, k * LANES : (k + 1) * LANES] = tail[:, k, :]
-    moves.append(pltpu.make_async_copy(wgrad_ref, wgrad_hbm, sems.at[2]))
-    moves[1].start()
     part = peers // 2
     for c in range(2):
         for s in range(c * part, (c + 1) * part):
@@ -155,6 +150,12 @@
         move = pltpu.make_async_copy(mirrors_ref.at[:, span], mirrors_hbm.at[:, span], sems.at[3 + c])
         move.start()
         moves.append(move)
+    tail = got_ref[:, rows:, :].astype(jnp.float32)
+    for k in range(wide):
+        wgrad_ref[:, k * LANES : (k + 1) * LANES] = tail[:, k, :]
+    move = pltpu.make_async_copy(wgrad_ref, wgrad_hbm, sems.at[2])
+    move.start()
+    moves.append(move)
     for move in moves:
         move.wait()
 

time: 84.6 us -> 84.6 us (level)
  no operation moved by 1% of the time
where the time goes in v9:
time: 84.6 us; the launch traced here: 84.3 us
  blocking collectives  77.9 us (92%)
  Pallas kernels  5.16 us (6%)
  between operations  1.3 us (2%)
    all_to_all x1, blocking collectives, body(): lax.all_to_all(message, 'dom', 0, 0, tiled=True, axis_index_groups=dom_gr...  37.3 us
    all_to_all x1, blocking collectives, body(): lax.all_to_all(answer, 'dom', 0, 0, tiled=True, axis_index_groups=dom_gro...  26 us
    all_to_all x1, blocking collectives, body(): lax.all_to_all(copies, 'feat', 0, 0, tiled=True, axis_index_groups=[order...  14.6 us
    pallas_call x1, Pallas kernels, body(): pl.pallas_call(stage_kernel, out_shape=(pltpu.VMEM((groups, rows, columns...  2.04 us

profile of v9, /device:TPU:1, one launch (start us, length us, event | category | flops | bytes accessed | tf_op | source)
XLA Modules:
  0.0 84.3 jit_solution(8291701962625516702)
XLA Ops:
  1.3 2.0 %stage.1 = (bf16[16,32,768]{2,1,0:T(8,128)(2,1)S(1)}, s32[96]{0:T(128)S(4)}, s32[96]{0:T(128)S(4)}, s32[32]{0:T(128)S(4)}, s32[32]{0:T(128)S(4)}, /*index=5*/bf1...) custom-call(bf16[32,768]{1,0:T(8,128)(2,1)} %grad_hbm.1, s32[96]{0:T(128)} %dst_hbm.1, ...), custom_call_target="tpu_custom_call" | custom-call | tf_op jit(solution)/shard_map/stage/pallas_call | solution.py:192
  3.3 14.6 %all_to_all.15.piece_ref = bf16[16,32,768]{2,1,0:T(8,128)(2,1)S(1)} all-to-all(bf16[16,32,768]{2,1,0:T(8,128)(2,1)S(1)} %get-tuple-element.20), channel_id=1, replica_groups={{10,0,1,2,3,4,5,6,7,8,9,11,12,13,14,15},{26,16,17,18,19,20,21,22,23,24,..., dimensions={0} | all-to-all | bytes 1572864 | tf_op jit(solution)/shard_map/gather_features/all_to_all | solution.py:218
  17.9 1.6 %partials.1 = bf16[32,19,2,128]{3,2,1,0:T(2,128)(2,1)S(1)} custom-call(s32[96]{0:T(128)S(4)} %get-tuple-element.17.dst_ref, s32[96]{0:T(128)S(4)} %get-tuple-element.18.place_ref, s32[32]{0:T(128)S(4)} %get-tuple-element.19.number_ref, bf16[16,32,768]{2,1,0:T(8,128)(2,1)S(1)} %all_to_all.15.piece_ref, bf16[32,512]{1,0:T(8,128)(2,1)S(1)} %get-tuple-element.21.weight_ref, ...), custom_call_target="tpu_custom_call" | custom-call | tf_op jit(solution)/shard_map/partials/pallas_call | solution.py:221
  19.5 37.3 %all_to_all.16.got_ref = bf16[32,19,2,128]{3,2,1,0:T(2,128)(2,1)S(1)} all-to-all(bf16[32,19,2,128]{3,2,1,0:T(2,128)(2,1)S(1)} %partials.1), channel_id=1, replica_groups={{304,0,16,32,48,64,80,96,112,128,144,160,176,192,208,224,240,256,272,28..., dimensions={0} | all-to-all | bytes 622592 | tf_op jit(solution)/shard_map/to_masters/all_to_all | solution.py:235
  56.8 0.7 masters.1
  57.5 26.0 %all_to_all.17.got_ref = bf16[32,9,4,128]{3,2,1,0:T(4,128)(2,1)S(1)} all-to-all(bf16[32,9,4,128]{3,2,1,0:T(4,128)(2,1)S(1)} %get-tuple-element.24), channel_id=1, replica_groups={{304,0,16,32,48,64,80,96,112,128,144,160,176,192,208,224,240,256,272,28..., dimensions={0} | all-to-all | bytes 589824 | tf_op jit(solution)/shard_map/to_mirrors/all_to_all | solution.py:248
  83.5 0.8 mirrors.1

commit v10 on v9

--- a/solution.py
+++ b/solution.py
@@ -34,7 +34,7 @@
         (weight_hbm, weight_ref), (agg_hbm, agg_ref), (tiles_hbm, tiles_ref),
     )
     moves = [pltpu.make_async_copy(a, b, sems.at[k]) for k, (a, b) in enumerate(pairs)]
-    for move in moves:
+    for move in (moves[0], moves[-1], *moves[1:-1]):
         move.start()
     peers = peer_ref.shape[0]
     tile_total = place_ref.shape[0]

time: 84.6 us -> 84.5 us (level)
  no operation moved by 1% of the time
where the time goes in v10:
time: 84.5 us; the launch traced here: 84.3 us
  blocking collectives  77.8 us (92%)
  Pallas kernels  5.13 us (6%)
  between operations  1.3 us (2%)
    all_to_all x1, blocking collectives, body(): lax.all_to_all(message, 'dom', 0, 0, tiled=True, axis_index_groups=dom_gr...  37.3 us
    all_to_all x1, blocking collectives, body(): lax.all_to_all(answer, 'dom', 0, 0, tiled=True, axis_index_groups=dom_gro...  26 us
    all_to_all x1, blocking collectives, body(): lax.all_to_all(copies, 'feat', 0, 0, tiled=True, axis_index_groups=[order...  14.6 us
    pallas_call x1, Pallas kernels, body(): pl.pallas_call(stage_kernel, out_shape=(pltpu.VMEM((groups, rows, columns...  2 us

profile of v10, /device:TPU:1, one launch (start us, length us, event | category | flops | bytes accessed | tf_op | source)
XLA Modules:
  0.0 84.3 jit_solution(5788594438630990888)
XLA Ops:
  1.3 2.0 %stage.1 = (bf16[16,32,768]{2,1,0:T(8,128)(2,1)S(1)}, s32[96]{0:T(128)S(4)}, s32[96]{0:T(128)S(4)}, s32[32]{0:T(128)S(4)}, s32[32]{0:T(128)S(4)}, /*index=5*/bf1...) custom-call(bf16[32,768]{1,0:T(8,128)(2,1)} %grad_hbm.1, s32[96]{0:T(128)} %dst_hbm.1, ...), custom_call_target="tpu_custom_call" | custom-call | tf_op jit(solution)/shard_map/stage/pallas_call | solution.py:192
  3.3 14.6 %all_to_all.15.piece_ref = bf16[16,32,768]{2,1,0:T(8,128)(2,1)S(1)} all-to-all(bf16[16,32,768]{2,1,0:T(8,128)(2,1)S(1)} %get-tuple-element.20), channel_id=1, replica_groups={{10,0,1,2,3,4,5,6,7,8,9,11,12,13,14,15},{26,16,17,18,19,20,21,22,23,24,..., dimensions={0} | all-to-all | bytes 1572864 | tf_op jit(solution)/shard_map/gather_features/all_to_all | solution.py:218
  17.9 1.6 %partials.1 = bf16[32,19,2,128]{3,2,1,0:T(2,128)(2,1)S(1)} custom-call(s32[96]{0:T(128)S(4)} %get-tuple-element.17.dst_ref, s32[96]{0:T(128)S(4)} %get-tuple-element.18.place_ref, s32[32]{0:T(128)S(4)} %get-tuple-element.19.number_ref, bf16[16,32,768]{2,1,0:T(8,128)(2,1)S(1)} %all_to_all.15.piece_ref, bf16[32,512]{1,0:T(8,128)(2,1)S(1)} %get-tuple-element.21.weight_ref, ...), custom_call_target="tpu_custom_call" | custom-call | tf_op jit(solution)/shard_map/partials/pallas_call | solution.py:221
  19.4 37.3 %all_to_all.16.got_ref = bf16[32,19,2,128]{3,2,1,0:T(2,128)(2,1)S(1)} all-to-all(bf16[32,19,2,128]{3,2,1,0:T(2,128)(2,1)S(1)} %partials.1), channel_id=1, replica_groups={{304,0,16,32,48,64,80,96,112,128,144,160,176,192,208,224,240,256,272,28..., dimensions={0} | all-to-all | bytes 622592 | tf_op jit(solution)/shard_map/to_masters/all_to_all | solution.py:235
  56.7 0.7 masters.1
  57.4 26.0 %all_to_all.17.got_ref = bf16[32,9,4,128]{3,2,1,0:T(4,128)(2,1)S(1)} all-to-all(bf16[32,9,4,128]{3,2,1,0:T(4,128)(2,1)S(1)} %get-tuple-element.24), channel_id=1, replica_groups={{304,0,16,32,48,64,80,96,112,128,144,160,176,192,208,224,240,256,272,28..., dimensions={0} | all-to-all | bytes 589824 | tf_op jit(solution)/shard_map/to_mirrors/all_to_all | solution.py:248
  83.4 0.8 mirrors.1
